TPU v7x, 32 devices: a whole 2x2x4 slice. The times are simulated.
32 devices in a mesh: users: 16 (over z, y, core), items: 2 (over x).
Axes of the slice: x: 2, y: 2, z: 4, core: 2. Of those that a mesh axis runs over, the one named last changes fastest.
Arguments:
- interactions: bfloat16 [3, 20480, 512], P(None, 'users', 'items')
- matchings: int32 [3], replicated, may hold values from 1 to 15, as said below
- user_shape: bfloat16 [20480, 128], P('users'), may hold values from 0.5 to 2
- item_shape: bfloat16 [8192, 128], P(('users', 'items')), may hold values from 0.5 to 2
Outputs:
- user_log: bfloat16 [20480, 128], P('users')
- item_log: bfloat16 [8192, 128], P(('users', 'items'))
Inputs may be any that keep to these rules, and one draw needn't show every extreme that they name: matchings[0] and matchings[1] are two different values of 1 to 14, and the last matching is 15.
All inputs are finite; a program needn't handle non-finite values.
Results may differ from a plain program's by a relative error of at most 0.0012.
The roundings to bfloat16 on the way count: a program that leaves them out, or rounds other values in their place, can miss the bound.
Values sent between devices are 32-bit elements; how exact they have to be, the bound alone decides.
No kernel may reach another device: no remote copies, remote signals or barrier semaphores. Data moves between devices by JAX's collectives and lax.ppermute only.
A program may use at most 64 MiB of HBM per device.

v0:
```python
import functools

import jax
import jax.numpy as jnp
from jax import lax
from jax.experimental import pallas as pl
from jax.experimental.pallas import tpu as pltpu
from jax.sharding import PartitionSpec as P

STRATA = 3
TILE = 128
F32 = jnp.float32
BF16 = jnp.bfloat16


def chunk_rows(rows):
    half = rows // 2 // TILE * TILE
    return [half, rows - half]


def psi_parts(x):
    small = x < 8.0
    w = jnp.where(small, x + 3.5, x - 0.5)
    q = x * (x + 3.0)
    q2 = q + 2.0
    bounded = jnp.minimum(w, 1e9)
    square = bounded * bounded
    steps = jnp.where(small, q * q2, 1.0)
    r = 1.0 / (square * steps)
    s = r * steps
    shift = (2.0 * x + 3.0) * (q + q2) * (r * square)
    g = s * (1.0 / 24.0 - s * (7.0 / 960.0 - s * (31.0 / 8064.0 - s * (127.0 / 30720.0))))
    return w, g - jnp.where(small, shift, 0.0)


def psi_any(x):
    mirrored = x < 0.5
    w, g = psi_parts(jnp.where(mirrored, 1.0 - x, x))
    value = jnp.log(w) + g
    t = x - jnp.floor(x + 0.5)
    u = 3.14159265358979 * t
    v = u * u
    sin = 1.0 / 6227020800.0
    for c in (-1.0 / 39916800.0, 1.0 / 362880.0, -1.0 / 5040.0, 1.0 / 120.0, -1.0 / 6.0, 1.0):
        sin = sin * v + c
    cos = -1.0 / 87178291200.0
    for c in (1.0 / 479001600.0, -1.0 / 3628800.0, 1.0 / 40320.0, -1.0 / 720.0, 1.0 / 24.0, -0.5, 1.0):
        cos = cos * v + c
    value = jnp.where(mirrored, value - 3.14159265358979 * cos / (sin * u), value)
    return jnp.where((x <= 0.0) & (x == jnp.floor(x)), jnp.nan, value)


LOWEST = 0.01


def above(low):
    return jnp.min(low) >= LOWEST


def folded(x):
    return x.reshape(x.shape[0] // 8, 8, x.shape[1])


def tiles(rows):
    step = TILE if rows % TILE == 0 else rows
    return [(at, step) for at in range(0, rows, step)]


def exp_tile(x, rte, general):
    shape = x.shape
    x = folded(x)
    if general:
        value = psi_any(x)
        if rte is not None:
            value = value - jnp.log(rte)[None]
        value = jnp.exp(value)
    else:
        w, g = psi_parts(x)
        value = w if rte is None else w * (1.0 / rte)[None]
        value = value * jnp.exp(g)
    mean = x if rte is None else x * (1.0 / rte)[None]
    return value.reshape(shape).astype(BF16), jnp.sum(mean, axis=0), jnp.min(x, axis=0)


def log_tile(x, rte, general):
    shape = x.shape
    x = folded(x)
    if general:
        value = psi_any(x) - jnp.log(rte)[None]
    else:
        w, g = psi_parts(x)
        value = (jnp.log(w) - jnp.log(rte)[None]) + g
    return value.reshape(shape).astype(BF16), jnp.min(x, axis=0)


def row_sum(x):
    return jnp.broadcast_to(jnp.sum(x, axis=0, keepdims=True), x.shape)


VMEM_SPEC = pl.BlockSpec(memory_space=pltpu.VMEM)
SMEM_SPEC = pl.BlockSpec(memory_space=pltpu.SMEM)
HBM_SPEC = pl.BlockSpec(memory_space=pltpu.HBM)
PARAMS = pltpu.CompilerParams(vmem_limit_bytes=24 * 2**20)


def prepare_kernel(matchings, item_shape, item, *choices, last):
    item[...] = item_shape[...].astype(F32)
    choices[0][0] = matchings[0] - 1
    for stratum in range(1, STRATA - 1):
        choices[stratum][0] = jnp.bitwise_xor(matchings[stratum - 1], matchings[stratum]) - 1
    choices[STRATA - 1][0] = jnp.bitwise_xor(matchings[STRATA - 2], last) - 1


def prepare_call(matchings, item_shape, last):
    out = pl.pallas_call(
        functools.partial(prepare_kernel, last=last),
        out_shape=[jax.ShapeDtypeStruct(item_shape.shape, F32)]
        + [jax.ShapeDtypeStruct((1,), jnp.int32)] * STRATA,
        in_specs=[SMEM_SPEC, VMEM_SPEC],
        out_specs=[VMEM_SPEC] + [SMEM_SPEC] * STRATA,
        compiler_params=PARAMS,
        name="prepare",
    )(matchings, item_shape)
    return out[0], [choice[0] for choice in out[1:]]


def start_kernel(shape, uexp, theta):
    rows, depth = shape.shape

    def body(general):
        def step(i, carry):
            total, low = carry
            place = pl.ds(pl.multiple_of(i * TILE, TILE), TILE)
            value, part, part_low = exp_tile(shape[place, :].astype(F32), None, general)
            uexp[place, :] = value
            return total + part, jnp.minimum(low, part_low)

        total, low = lax.fori_loop(
            0, rows // TILE, step, (jnp.zeros((8, depth), F32), jnp.ones((8, depth), F32)))
        theta[...] = total
        return low

    low = body(False)

    @pl.when(jnp.logical_not(above(low)))
    def _():
        body(True)


def start_call(user_shape):
    rows, depth = user_shape.shape
    return pl.pallas_call(
        start_kernel,
        out_shape=[jax.ShapeDtypeStruct((rows, depth), BF16), jax.ShapeDtypeStruct((8, depth), F32)],
        in_specs=[VMEM_SPEC],
        out_specs=[VMEM_SPEC] * 2,
        compiler_params=PARAMS,
        cost_estimate=pl.CostEstimate(
            flops=40 * rows * depth, bytes_accessed=rows * depth * 4, transcendentals=2 * rows * depth),
        name="user_start",
    )(user_shape)


def stratum_kernel(names, *refs, stratum, at, rows, items, factor, first, last):
    ref = dict(zip(names, refs))
    sems = ref["sems"]
    copies = {}

    def fetch(name, source, target):
        copies[name] = pltpu.make_async_copy(source, target, sems.at[len(copies)])
        copies[name].start()

    place = pl.ds(at, rows)
    if first or last:
        fetch("item", ref["item"], ref["item_in"])
    if stratum == 0:
        fetch("uexp", ref["uexp_all"].at[place, :], ref["uexp"])
    if stratum == 1:
        fetch("shape", ref["user_shape"].at[place, :], ref["shape_in"])
    fetch("counts", ref["interactions"].at[stratum, place, :], ref["counts"])
    upart, uexp, counts, ratios = ref["upart"], ref["uexp"], ref["counts"], ref["ratios"]
    extra = 8 if first else 0

    def wait(name, general):
        if not general:
            copies[name].wait()

    def body(general):
        lows = []
        theta = None
        if stratum > 0:
            if first:
                beta = row_sum(ref["acc"][0:8, :] + ref["recv"][0:8, :])
                old = 1.0 if stratum == 1 else ref["rte_old"][...]
                rte = 0.5 * old + 0.5 * (0.3 + factor * beta)
                ref["rte_new"][...] = rte
            else:
                rte = ref["rte"][...]
            lows.append(rte)
            if stratum == 1:
                wait("shape", general)
            for t, step in tiles(rows):
                old = ref["shape_in"][t:t + step, :].astype(F32) if stratum == 1 else ref["shp_old"][t:t + step, :]
                stat = ref["acc"][extra + t:extra + t + step, :] + ref["recv"][extra + t:extra + t + step, :]
                shp = 0.5 * old + 0.5 * (0.3 + factor * stat)
                ref["shp_new"][t:t + step, :] = shp
                value, part, low = exp_tile(shp, rte, general)
                uexp[t:t + step, :] = value
                theta = part if theta is None else theta + part
                lows.append(low)
            if not first:
                theta = theta + ref["theta"][...]
        elif last:
            theta = ref["theta"][...]

        if first or last:
            wait("item", general)
            item = ref["item_in"]
            item_rte = None if stratum == 0 else item[items:items + 8, :]
        if first:
            value, sums, low = exp_tile(item[0:items, :], item_rte, general)
            ref["item_exp_new"][...] = value
            upart[0:8, :] = sums
            lows.append(low)
            if item_rte is not None:
                lows.append(item_rte)
            item_exp = value
        else:
            item_exp = ref["item_exp"][...]

        if stratum == 0:
            wait("uexp", general)
        wait("counts", general)
        for t, step in tiles(rows):
            u = uexp[t:t + step, :]
            denominator = lax.dot_general(u, item_exp, (((1,), (1,)), ((), ())), preferred_element_type=F32)
            ratio = (counts[t:t + step, :].astype(F32) / denominator).astype(BF16)
            ratios[t:t + step, :] = ratio
            upart[extra + t:extra + t + step, :] = u.astype(F32) * jnp.dot(
                ratio, item_exp, preferred_element_type=F32)
        istat = lax.dot_general(ratios[...], uexp[...], (((0,), (0,)), ((), ())), preferred_element_type=F32)
        if not first:
            istat = istat + ref["istat"][...]
        if last:
            old = 1.0 if item_rte is None else item_rte
            ref["item_new"][0:items, :] = 0.5 * item[0:items, :] + 0.5 * (
                0.3 + factor * (item_exp.astype(F32) * istat))
            ref["item_new"][items:items + 8, :] = 0.5 * old + 0.5 * (0.3 + factor * row_sum(theta))
        else:
            ref["istat_new"][...] = istat
            if stratum > 0:
                ref["theta_new"][...] = theta
        return functools.reduce(jnp.minimum, lows) if lows else None

    low = body(False)
    if low is not None:

        @pl.when(jnp.logical_not(above(low)))
        def _():
            body(True)


def stratum_call(stratum, at, rows, items, depth, factor, first, last, operands):
    extra = 8 if first else 0
    outs = {"upart": ((rows + extra, depth), F32)}
    if stratum > 0:
        outs["shp_new"] = ((rows, depth), F32)
    if first and stratum > 0:
        outs["rte_new"] = ((8, depth), F32)
    if first:
        outs["item_exp_new"] = ((items, depth), BF16)
    if last:
        outs["item_new"] = ((items + 8, depth), F32)
    else:
        outs["istat_new"] = ((items, depth), F32)
        if stratum > 0:
            outs["theta_new"] = ((8, depth), F32)
    scratch = {
        "counts": pltpu.VMEM((rows, items), BF16),
        "ratios": pltpu.VMEM((rows, items), BF16),
        "uexp": pltpu.VMEM((rows, depth), BF16),
        "sems": pltpu.SemaphoreType.DMA((3,)),
    }
    if stratum == 1:
        scratch["shape_in"] = pltpu.VMEM((rows, depth), BF16)
    if first or last:
        scratch["item_in"] = pltpu.VMEM(operands["item"].shape, F32)
    in_hbm = ("interactions", "user_shape", "uexp_all", "item")
    names = list(operands) + list(outs) + list(scratch)
    kernel = functools.partial(
        stratum_kernel, names, stratum=stratum, at=at, rows=rows, items=items,
        factor=factor, first=first, last=last)
    results = pl.pallas_call(
        kernel,
        out_shape=[jax.ShapeDtypeStruct(*spec) for spec in outs.values()],
        in_specs=[HBM_SPEC if name in in_hbm else VMEM_SPEC for name in operands],
        out_specs=[VMEM_SPEC] * len(outs),
        scratch_shapes=list(scratch.values()),
        compiler_params=PARAMS,
        cost_estimate=pl.CostEstimate(
            flops=6 * rows * items * depth, bytes_accessed=rows * (items * 2 + depth * 16),
            transcendentals=rows * (depth + items)),
        name=f"stratum{stratum}_at{at}",
    )(*operands.values())
    return dict(zip(outs, results))


def user_log_kernel(*refs, at, rows, factor, first, filled):
    acc, recv, shp_old, rte_in = refs[:4]
    rest = refs[5:] if filled else refs[4:]
    if first:
        out, rte_out, block, sem = rest
        beta = row_sum(acc[0:8, :] + recv[0:8, :])
        rte = 0.5 * rte_in[...] + 0.5 * (0.3 + factor * beta)
        rte_out[...] = rte
    else:
        out, block, sem = rest
        rte = rte_in[...]
    extra = 8 if first else 0

    def body(general):
        low = rte
        for t, step in tiles(rows):
            stat = acc[extra + t:extra + t + step, :] + recv[extra + t:extra + t + step, :]
            shp = 0.5 * shp_old[t:t + step, :] + 0.5 * (0.3 + factor * stat)
            block[t:t + step, :], part_low = log_tile(shp, rte, general)
            low = jnp.minimum(low, part_low)
        return low

    low = body(False)

    @pl.when(jnp.logical_not(above(low)))
    def _():
        body(True)

    copy = pltpu.make_async_copy(block, out.at[pl.ds(at, rows), :], sem)
    copy.start()
    copy.wait()


def user_log_call(at, rows, total, depth, factor, first, operands, filled):
    out_shape = [jax.ShapeDtypeStruct((total, depth), BF16)]
    out_specs = [HBM_SPEC]
    if first:
        out_shape.append(jax.ShapeDtypeStruct((8, depth), F32))
        out_specs.append(VMEM_SPEC)
    operands = list(operands)
    in_specs = [VMEM_SPEC] * 4
    if filled is not None:
        operands.append(filled)
        in_specs.append(HBM_SPEC)
    return pl.pallas_call(
        functools.partial(user_log_kernel, at=at, rows=rows, factor=factor, first=first,
                          filled=filled is not None),
        out_shape=out_shape,
        in_specs=in_specs,
        out_specs=out_specs,
        input_output_aliases={} if filled is None else {4: 0},
        scratch_shapes=[pltpu.VMEM((rows, depth), BF16), pltpu.SemaphoreType.DMA],
        compiler_params=PARAMS,
        cost_estimate=pl.CostEstimate(
            flops=40 * rows * depth, bytes_accessed=rows * depth * 14, transcendentals=rows * depth),
        name=f"user_log_at{at}",
    )(*operands)


def item_log_kernel(item, out, *, items):
    rte = item[items:items + 8, :]

    def body(general):
        out[...], low = log_tile(item[0:items, :], rte, general)
        return low

    low = body(False)

    @pl.when(jnp.logical_not(above(jnp.minimum(low, rte))))
    def _():
        body(True)


def item_log_call(item, items, depth):
    return pl.pallas_call(
        functools.partial(item_log_kernel, items=items),
        out_shape=jax.ShapeDtypeStruct((items, depth), BF16),
        in_specs=[VMEM_SPEC],
        out_specs=VMEM_SPEC,
        compiler_params=PARAMS,
        cost_estimate=pl.CostEstimate(
            flops=40 * items * depth, bytes_accessed=items * depth * 6, transcendentals=items * depth),
        name="item_log",
    )(item)


def swapped(value, axis, mask):
    return lax.ppermute(value, axis, [(a, a ^ mask) for a in range(lax.axis_size(axis))])


def moved(choice, value, beside=None, operands=()):
    def branch(mask, value, *operands):
        arrived = swapped(value, "users", mask)
        return (arrived,) if beside is None else (arrived, *beside(*operands))

    choices = [functools.partial(branch, mask) for mask in range(1, lax.axis_size("users"))]
    return lax.switch(choice, choices, value, *operands)


def exchanged(value):
    size = lax.axis_size("items")
    if size == 1:
        return value, jnp.zeros_like(value)
    mask = 1
    while mask * 2 < size:
        value = value + swapped(value, "items", mask)
        mask *= 2
    return value, swapped(value, "items", mask)


def per_device(interactions, matchings, user_shape, item_shape):
    group = lax.axis_size("users")
    factor = float(group)
    users, depth = user_shape.shape
    items = item_shape.shape[0]
    sizes = chunk_rows(users)
    starts = [sum(sizes[:i]) for i in range(len(sizes))]
    count = len(sizes)

    item, choices = prepare_call(matchings, item_shape, group - 1)
    item, uexp, theta = moved(choices[0], item, start_call, (user_shape,))
    rte = None
    shp = [None] * count
    sums = [None] * count
    for stratum in range(STRATA):
        carried = {"theta": theta}
        for i, (at, rows) in enumerate(zip(starts, sizes)):
            first, last = i == 0, i == count - 1
            operands = {"interactions": interactions}
            if stratum == 0:
                operands["uexp_all"] = uexp
            else:
                operands["acc"], operands["recv"] = sums[i]
                if stratum == 1:
                    operands["user_shape"] = user_shape
                else:
                    operands["shp_old"] = shp[i]
                if not first:
                    operands["rte"] = rte
                elif stratum > 1:
                    operands["rte_old"] = rte
            if first or last:
                operands["item"] = item
            if not first:
                operands["item_exp"] = carried["item_exp"]
                operands["istat"] = carried["istat"]
            if (stratum > 0 and not first) or (stratum == 0 and last):
                operands["theta"] = carried["theta"]
            out = stratum_call(stratum, at, rows, items, depth, factor, first, last, operands)
            shp[i] = out.get("shp_new")
            sums[i] = exchanged(out["upart"])
            if first:
                rte = out.get("rte_new")
                carried["item_exp"] = out["item_exp_new"]
            if last:
                item = out["item_new"]
            else:
                carried["istat"] = out["istat_new"]
                if stratum > 0:
                    carried["theta"] = out["theta_new"]
        if stratum + 1 < STRATA:
            item, = moved(choices[stratum + 1], item)
        else:
            item = swapped(item, "users", group - 1)
    item_log = item_log_call(item, items, depth)
    user_log = None
    for i, (at, rows) in enumerate(zip(starts, sizes)):
        out = user_log_call(at, rows, users, depth, factor, i == 0, (*sums[i], shp[i], rte), user_log)
        user_log = out[0]
        if i == 0:
            rte = out[1]
    return user_log, item_log


def solution(mesh):
    placed = (P(None, "users", "items"), P(), P("users", None), P(("users", "items"), None))
    return jax.shard_map(
        per_device,
        mesh=mesh,
        in_specs=placed,
        out_specs=(P("users", None), P(("users", "items"), None)),
        check_vma=False,
    )
```

profile of v0, /device:TPU:0, one launch (start us, length us, event | category | flops | bytes accessed | tf_op | source)
XLA Modules:
  0.0 60.5 jit_solution(1533084976779692621)
XLA Ops:
  0.6 0.0 copy-start.5
  0.6 0.8 %copy-done.5 = bf16[256,128]{1,0:T(8,128)(2,1)S(1)} copy-done((bf16[256,128]{1,0:T(8,128)(2,1)S(1)}, bf16[256,128]{1,0:T(8,128)(2,1)}, u32[]{:S(2)}) %copy-start.5) | copy-done | bytes 65560
  1.5 0.0 copy-start.6
  1.5 0.7 %copy-done.6 = s32[3]{0:T(128)S(1)} copy-done((s32[3]{0:T(128)S(1)}, s32[3]{0:T(128)}, u32[]{:S(2)}) %copy-start.6) | copy-done | bytes 36
  2.1 1.1 %prepare.1 = (f32[256,128]{1,0:T(8,128)S(1)}, s32[1]{0:T(128)}, s32[1]{0:T(128)}, s32[1]{0:T(128)}) custom-call(s32[3]{0:T(128)S(1)} %copy-done.6, bf16[256,128]{1,0:T(8,128)(2,1)S(1)} %copy-done.5), custom_call_target="tpu_custom_call" | custom-call | tf_op jit(solution)/shard_map/prepare/pallas_call | solution.py:115
  3.9 0.0 copy-start
  3.9 2.6 %conditional.3 = (f32[256,128]{1,0:T(8,128)}, bf16[1280,128]{1,0:T(8,128)(2,1)S(1)}, f32[8,128]{1,0:T(8,128)S(1)}) conditional(s32[]{:T(128)} %bitcast, (f32[256,128]{1,0:T(8,128)S(1)}, bf16[1280,128]{1,0:T(8,128)(2,1)}) %tuple.158, (f32[256,128]{1,0:T(8,128)S(1)}, bf16[1280,128]{1,0:T(8,128)(2,1)}) %tuple.158, ...), branch_computations={%region_0.0_spmd, %region_1.0_spmd, %region_2.0_spmd, %region_3.0_... | conditional | flops 6553600 | bytes 1179712 | solution.py:404
  3.9 0.5 collective-permute-start
  4.4 2.0 %user_start.15 = (bf16[1280,128]{1,0:T(8,128)(2,1)S(1)}, f32[8,128]{1,0:T(8,128)S(1)}) custom-call(bf16[1280,128]{1,0:T(8,128)(2,1)} %get-tuple-element.123.shape), custom_call_target="tpu_custom_call" | custom-call | flops 6553600 | bytes 655360 | tf_op jit(solution)/shard_map/cond/branch_0_fun/user_start/pallas_call | solution.py:152
  6.4 0.0 collective-permute-done
  6.4 0.0 copy-start.7
  6.4 0.0 copy-done
  6.5 1.9 %stratum0_at0.1 = (f32[648,128]{1,0:T(8,128)S(1)}, bf16[256,128]{1,0:T(8,128)(2,1)S(1)}, f32[256,128]{1,0:T(8,128)S(1)}) custom-call(bf16[3,1280,256]{2,1,0:T(8,128)(2,1)S(1)} %copy-done, bf16[1280,128]{1,0:T(8,128)(2,1)S(1)} %get-tuple-element.218.refs_1_, f32[256,128]{1,0:T(8,128)} %get-tuple-element.219.refs_2_), custom_call_target="tpu_custom_call" | custom-call | flops 125829120 | bytes 1638400 | tf_op jit(solution)/shard_map/stratum0_at0/pallas_call | solution.py:293
  8.3 0.0 copy-done.7
  8.3 2.7 %collective-permute-start.46 = (f32[648,128]{1,0:T(8,128)S(1)}, f32[648,128]{1,0:T(8,128)S(1)}, u32[]{:S(2)}, u32[]{:S(2)}) collective-permute-start(f32[648,128]{1,0:T(8,128)S(1)} %get-tuple-element.224.refs_1_), channel_id=1, source_target_pairs={{0,1},{1,0},{2,3},{3,2},{4,5},{5,4},{6,7},{7,6},{8,9},{9,8},{10,11... | collective-permute-start | bytes 995336 | tf_op jit(solution)/shard_map/ppermute | solution.py:395
  11.0 1.7 %stratum0_at640.1 = (f32[640,128]{1,0:T(8,128)S(1)}, f32[264,128]{1,0:T(8,128)S(1)}) custom-call(bf16[3,1280,256]{2,1,0:T(8,128)(2,1)S(1)} %copy-done, bf16[1280,128]{1,0:T(8,128)(2,1)} %copy-done.7, f32[256,128]{1,0:T(8,128)} %get-tuple-element.219.refs_2_, bf16[256,128]{1,0:T(8,128)(2,1)S(1)} %get-tuple-element.220.refs_3_, ...), custom_call_target="tpu_custom_call" | custom-call | flops 125829120 | bytes 1638400 | tf_op jit(solution)/shard_map/stratum0_at640/pallas_call | solution.py:293
  12.7 0.0 copy-start.3
  12.7 0.1 collective-permute-start.45
  13.4 10.0 %conditional.4 = (f32[264,128]{1,0:T(8,128)}) conditional(s32[]{:T(128)} %bitcast.1, f32[264,128]{1,0:T(8,128)S(1)} %get-tuple-element.226, f32[264,128]{1,0:T(8,128)S(1)} %get-tuple-element.226, f32[264,128]{1,0:T(8,128)S(1)} %get-tuple-element.226, f32[264,128]{1,0:T(8,128)S(1)} %get-tuple-element.226, ...), branch_computations={%region_15.0_spmd, %region_16.0_spmd, %region_17.0_spmd, %region_1... | conditional | bytes 540720 | solution.py:404
  13.4 3.5 %collective-permute-start.25 = (f32[264,128]{1,0:T(8,128)S(1)}, f32[264,128]{1,0:T(8,128)}, u32[]{:S(2)}, u32[]{:S(2)}) collective-permute-start(f32[264,128]{1,0:T(8,128)S(1)} %param.25), channel_id=1, source_target_pairs={{0,22},{2,20},{4,18},{6,16},{8,30},{10,28},{12,26},{14,24},{16,6},... | collective-permute-start | bytes 405512 | tf_op jit(solution)/shard_map/cond/branch_10_fun/ppermute | solution.py:395
  16.9 6.5 %collective-permute-done.25 = f32[264,128]{1,0:T(8,128)} collective-permute-done((f32[264,128]{1,0:T(8,128)S(1)}, f32[264,128]{1,0:T(8,128)}, u32[]{:S(2)}, u32[]{:S(2)}) %collective-permute-start.25) | collective-permute-done | bytes 135200 | tf_op jit(solution)/shard_map/cond/branch_10_fun/ppermute | solution.py:395
  23.4 0.0 collective-permute-done.46.refs_2_
  23.4 2.5 %stratum1_at0.1 = (f32[648,128]{1,0:T(8,128)S(1)}, f32[640,128]{1,0:T(8,128)S(1)}, f32[8,128]{1,0:T(8,128)S(1)}, bf16[256,128]{1,0:T(8,128)(2,1)S(1)}, f32[256,128]{1,0:T(8,128)S(1)}, /*index=5*/f32[8,128]{1,0:T(8,128)S(1)}) custom-call(bf16[3,1280,256]{2,1,0:T(8,128)(2,1)S(1)} %copy-done, f32[648,128]{1,0:T(8,128)S(1)} %get-tuple-element.224.refs_1_, ...), custom_call_target="tpu_custom_call" | custom-call | flops 125829120 | bytes 1638400 | tf_op jit(solution)/shard_map/stratum1_at0/pallas_call | solution.py:293
  25.9 0.0 copy-start.1
  25.9 2.5 %collective-permute-start.48 = (f32[648,128]{1,0:T(8,128)S(1)}, f32[648,128]{1,0:T(8,128)S(1)}, u32[]{:S(2)}, u32[]{:S(2)}) collective-permute-start(f32[648,128]{1,0:T(8,128)S(1)} %get-tuple-element.233.refs_1_), channel_id=1, source_target_pairs={{0,1},{1,0},{2,3},{3,2},{4,5},{5,4},{6,7},{7,6},{8,9},{9,8},{10,11... | collective-permute-start | bytes 995336 | tf_op jit(solution)/shard_map/ppermute | solution.py:395
  28.4 0.0 collective-permute-done.45.refs_2_
  28.4 0.0 copy-done.3
  28.4 1.0 %copy-done.4 = f32[640,128]{1,0:T(8,128)S(1)} copy-done((f32[640,128]{1,0:T(8,128)S(1)}, f32[640,128]{1,0:T(8,128)}, u32[]{:S(2)}) %copy-start.4) | copy-done | bytes 327704
  29.4 3.1 %stratum1_at640.1 = (f32[640,128]{1,0:T(8,128)S(1)}, f32[640,128]{1,0:T(8,128)S(1)}, f32[264,128]{1,0:T(8,128)S(1)}) custom-call(bf16[3,1280,256]{2,1,0:T(8,128)(2,1)S(1)} %copy-done, f32[640,128]{1,0:T(8,128)S(1)} %copy-done.4, f32[640,128]{1,0:T(8,128)} %collective-permute-done.45.refs_2_, bf16[1280,128]{1,0:T(8,128)(2,1)} %refs_3_.3, ...), custom_call_target="tpu_custom_call" | custom-call | flops 125829120 | bytes 1638400 | tf_op jit(solution)/shard_map/stratum1_at640/pallas_call | solution.py:293
  32.6 0.0 copy-done.1
  32.6 0.1 collective-permute-start.47
  33.4 6.1 %conditional.5 = (f32[264,128]{1,0:T(8,128)}) conditional(s32[]{:T(128)} %bitcast.2, f32[264,128]{1,0:T(8,128)S(1)} %get-tuple-element.236, f32[264,128]{1,0:T(8,128)S(1)} %get-tuple-element.236, f32[264,128]{1,0:T(8,128)S(1)} %get-tuple-element.236, f32[264,128]{1,0:T(8,128)S(1)} %get-tuple-element.236, ...), branch_computations={%region_30.0_spmd, %region_31.0_spmd, %region_32.0_spmd, %region_3... | conditional | bytes 540720 | solution.py:404
  33.4 0.6 %collective-permute-start.34 = (f32[264,128]{1,0:T(8,128)S(1)}, f32[264,128]{1,0:T(8,128)}, u32[]{:S(2)}, u32[]{:S(2)}) collective-permute-start(f32[264,128]{1,0:T(8,128)S(1)} %param.34), channel_id=1, source_target_pairs={{0,10},{2,8},{4,14},{6,12},{8,2},{10,0},{12,6},{14,4},{16,26},{18,... | collective-permute-start | bytes 405512 | tf_op jit(solution)/shard_map/cond/branch_4_fun/ppermute | solution.py:395
  34.0 5.4 %collective-permute-done.34 = f32[264,128]{1,0:T(8,128)} collective-permute-done((f32[264,128]{1,0:T(8,128)S(1)}, f32[264,128]{1,0:T(8,128)}, u32[]{:S(2)}, u32[]{:S(2)}) %collective-permute-start.34) | collective-permute-done | bytes 135200 | tf_op jit(solution)/shard_map/cond/branch_4_fun/ppermute | solution.py:395
  39.4 0.0 collective-permute-done.48.refs_2_
  39.4 1.0 %copy-done.2 = f32[640,128]{1,0:T(8,128)S(1)} copy-done((f32[640,128]{1,0:T(8,128)S(1)}, f32[640,128]{1,0:T(8,128)}, u32[]{:S(2)}) %copy-start.2) | copy-done | bytes 327704
  40.4 1.8 %stratum2_at0.1 = (f32[648,128]{1,0:T(8,128)S(1)}, f32[640,128]{1,0:T(8,128)S(1)}, f32[8,128]{1,0:T(8,128)S(1)}, bf16[256,128]{1,0:T(8,128)(2,1)S(1)}, f32[256,128]{1,0:T(8,128)S(1)}, /*index=5*/f32[8,128]{1,0:T(8,128)S(1)}) custom-call(bf16[3,1280,256]{2,1,0:T(8,128)(2,1)S(1)} %copy-done, f32[648,128]{1,0:T(8,128)S(1)} %get-tuple-element.233.refs_1_, ...), custom_call_target="tpu_custom_call" | custom-call | flops 125829120 | bytes 1638400 | tf_op jit(solution)/shard_map/stratum2_at0/pallas_call | solution.py:293
  42.2 1.8 %collective-permute-start.50 = (f32[648,128]{1,0:T(8,128)S(1)}, f32[648,128]{1,0:T(8,128)S(1)}, u32[]{:S(2)}, u32[]{:S(2)}) collective-permute-start(f32[648,128]{1,0:T(8,128)S(1)} %get-tuple-element.243.refs_0_), channel_id=1, source_target_pairs={{0,1},{1,0},{2,3},{3,2},{4,5},{5,4},{6,7},{7,6},{8,9},{9,8},{10,11... | collective-permute-start | bytes 995336 | tf_op jit(solution)/shard_map/ppermute | solution.py:395
  44.0 0.0 collective-permute-done.47.refs_2_
  44.0 2.6 %stratum2_at640.1 = (f32[640,128]{1,0:T(8,128)S(1)}, f32[640,128]{1,0:T(8,128)S(1)}, f32[264,128]{1,0:T(8,128)S(1)}) custom-call(bf16[3,1280,256]{2,1,0:T(8,128)(2,1)S(1)} %copy-done, f32[640,128]{1,0:T(8,128)S(1)} %get-tuple-element.231.refs_1_, f32[640,128]{1,0:T(8,128)} %collective-permute-done.47.refs_2_, f32[640,128]{1,0:T(8,128)S(1)} %get-tuple-element.232.refs_3_, ...), custom_call_target="tpu_custom_call" | custom-call | flops 125829120 | bytes 1638400 | tf_op jit(solution)/shard_map/stratum2_at640/pallas_call | solution.py:293
  46.6 1.5 %collective-permute-start.49 = (f32[640,128]{1,0:T(8,128)S(1)}, f32[640,128]{1,0:T(8,128)S(1)}, u32[]{:S(2)}, u32[]{:S(2)}) collective-permute-start(f32[640,128]{1,0:T(8,128)S(1)} %get-tuple-element.241.refs_0_), channel_id=1, source_target_pairs={{0,1},{1,0},{2,3},{3,2},{4,5},{5,4},{6,7},{7,6},{8,9},{9,8},{10,11... | collective-permute-start | bytes 983048 | tf_op jit(solution)/shard_map/ppermute | solution.py:395
  48.0 3.3 %collective-permute-start.51 = (f32[264,128]{1,0:T(8,128)S(1)}, f32[264,128]{1,0:T(8,128)S(1)}, u32[]{:S(2)}, u32[]{:S(2)}) collective-permute-start(f32[264,128]{1,0:T(8,128)S(1)} %get-tuple-element.247), channel_id=1, source_target_pairs={{0,30},{2,28},{4,26},{6,24},{8,22},{10,20},{12,18},{14,16},{16,14}... | collective-permute-start | bytes 405512 | tf_op jit(solution)/shard_map/ppermute | solution.py:395
  51.4 4.9 %collective-permute-done.51.item = f32[264,128]{1,0:T(8,128)S(1)} collective-permute-done((f32[264,128]{1,0:T(8,128)S(1)}, f32[264,128]{1,0:T(8,128)S(1)}, u32[]{:S(2)}, u32[]{:S(2)}) %collective-permute-start.51) | collective-permute-done | bytes 135200 | tf_op jit(solution)/shard_map/ppermute | solution.py:395
  56.2 1.1 %item_log.1 = bf16[256,128]{1,0:T(8,128)(2,1)} custom-call(f32[264,128]{1,0:T(8,128)S(1)} %collective-permute-done.51.item), custom_call_target="tpu_custom_call" | custom-call | flops 1310720 | bytes 196608 | tf_op jit(solution)/shard_map/item_log/pallas_call | solution.py:382
  57.4 0.0 collective-permute-done.50.refs_1_
  57.4 1.3 %user_log_at0.1 = (bf16[1280,128]{1,0:T(8,128)(2,1)}, f32[8,128]{1,0:T(8,128)S(1)}) custom-call(f32[648,128]{1,0:T(8,128)S(1)} %get-tuple-element.243.refs_0_, f32[648,128]{1,0:T(8,128)S(1)} %collective-permute-done.50.refs_1_, f32[640,128]{1,0:T(8,128)S(1)} %get-tuple-element.244.refs_2_, f32[8,128]{1,0:T(8,128)S(1)} %get-tuple-element.237.refs_4_.refs_3_), custom_call_target="tpu_custom_call" | custom-call | flops 3276800 | bytes 1146880 | tf_op jit(solution)/shard_map/user_log_at0/pallas_call | solution.py:352
  58.7 0.4 collective-permute-done.49.refs_1_
  59.1 1.3 %user_log_at640.1 = bf16[1280,128]{1,0:T(8,128)(2,1)} custom-call(f32[640,128]{1,0:T(8,128)S(1)} %get-tuple-element.241.refs_0_, f32[640,128]{1,0:T(8,128)S(1)} %collective-permute-done.49.refs_1_, f32[640,128]{1,0:T(8,128)S(1)} %get-tuple-element.242.refs_2_, f32[8,128]{1,0:T(8,128)S(1)} %get-tuple-element.245.refs_3_, ...), custom_call_target="tpu_custom_call", output_to_operand_aliasing={{}: (4, {})} | custom-call | flops 3276800 | bytes 1146880 | tf_op jit(solution)/shard_map/user_log_at640/pallas_call | solution.py:352
  (2 shorter events, 0.0 us)
Async XLA Ops:
  0.6 0.8 %copy-start.5 = (bf16[256,128]{1,0:T(8,128)(2,1)S(1)}, bf16[256,128]{1,0:T(8,128)(2,1)}, u32[]{:S(2)}) copy-start(bf16[256,128]{1,0:T(8,128)(2,1)} %item_shape.1) | copy-start | bytes 196612
  1.5 0.7 %copy-start.6 = (s32[3]{0:T(128)S(1)}, s32[3]{0:T(128)}, u32[]{:S(2)}) copy-start(s32[3]{0:T(128)} %matchings.1) | copy-start | bytes 40
  3.9 2.6 %copy-start = (bf16[3,1280,256]{2,1,0:T(8,128)(2,1)S(1)}, bf16[3,1280,256]{2,1,0:T(8,128)(2,1)}, u32[]{:S(2)}) copy-start(bf16[3,1280,256]{2,1,0:T(8,128)(2,1)} %refs_0_.11) | copy-start | bytes 5898244
  3.9 2.5 %collective-permute-start = (f32[256,128]{1,0:T(8,128)S(1)}, f32[256,128]{1,0:T(8,128)}, u32[]{:S(2)}, u32[]{:S(2)}) collective-permute-start(f32[256,128]{1,0:T(8,128)S(1)} %get-tuple-element.122), channel_id=1, source_target_pairs={{0,2},{2,0},{4,6},{6,4},{8,10},{10,8},{12,14},{14,12},{16,18},{18,... | collective-permute-start | bytes 393224 | tf_op jit(solution)/shard_map/cond/branch_0_fun/ppermute | solution.py:395
  6.4 1.9 %copy-start.7 = (bf16[1280,128]{1,0:T(8,128)(2,1)}, bf16[1280,128]{1,0:T(8,128)(2,1)S(1)}, u32[]{:S(2)}) copy-start(bf16[1280,128]{1,0:T(8,128)(2,1)S(1)} %get-tuple-element.218.refs_1_) | copy-start | bytes 983044
  8.3 15.0 %collective-permute-start.46 = (f32[648,128]{1,0:T(8,128)S(1)}, f32[648,128]{1,0:T(8,128)S(1)}, u32[]{:S(2)}, u32[]{:S(2)}) collective-permute-start(f32[648,128]{1,0:T(8,128)S(1)} %get-tuple-element.224.refs_1_), channel_id=1, source_target_pairs={{0,1},{1,0},{2,3},{3,2},{4,5},{5,4},{6,7},{7,6},{8,9},{9,8},{10,11... | collective-permute-start | bytes 995336 | tf_op jit(solution)/shard_map/ppermute | solution.py:395
  12.7 15.7 %copy-start.3 = (f32[640,128]{1,0:T(8,128)}, f32[640,128]{1,0:T(8,128)S(1)}, u32[]{:S(2)}) copy-start(f32[640,128]{1,0:T(8,128)S(1)} %get-tuple-element.223.refs_1_) | copy-start | bytes 983044
  12.7 15.7 %collective-permute-start.45 = (f32[640,128]{1,0:T(8,128)S(1)}, f32[640,128]{1,0:T(8,128)}, u32[]{:S(2)}, u32[]{:S(2)}) collective-permute-start(f32[640,128]{1,0:T(8,128)S(1)} %get-tuple-element.223.refs_1_), channel_id=1, source_target_pairs={{0,1},{1,0},{2,3},{3,2},{4,5},{5,4},{6,7},{7,6},{8,9},{9,8},{10,11... | collective-permute-start | bytes 983048 | tf_op jit(solution)/shard_map/ppermute | solution.py:395
  13.4 10.0 %collective-permute-start.25 = (f32[264,128]{1,0:T(8,128)S(1)}, f32[264,128]{1,0:T(8,128)}, u32[]{:S(2)}, u32[]{:S(2)}) collective-permute-start(f32[264,128]{1,0:T(8,128)S(1)} %param.25), channel_id=1, source_target_pairs={{0,22},{2,20},{4,18},{6,16},{8,30},{10,28},{12,26},{14,24},{16,6},... | collective-permute-start | bytes 405512 | tf_op jit(solution)/shard_map/cond/branch_10_fun/ppermute | solution.py:395
  25.9 6.7 %copy-start.1 = (f32[640,128]{1,0:T(8,128)}, f32[640,128]{1,0:T(8,128)S(1)}, u32[]{:S(2)}) copy-start(f32[640,128]{1,0:T(8,128)S(1)} %get-tuple-element.234.refs_3_) | copy-start | bytes 983044
  25.9 13.5 %collective-permute-start.48 = (f32[648,128]{1,0:T(8,128)S(1)}, f32[648,128]{1,0:T(8,128)S(1)}, u32[]{:S(2)}, u32[]{:S(2)}) collective-permute-start(f32[648,128]{1,0:T(8,128)S(1)} %get-tuple-element.233.refs_1_), channel_id=1, source_target_pairs={{0,1},{1,0},{2,3},{3,2},{4,5},{5,4},{6,7},{7,6},{8,9},{9,8},{10,11... | collective-permute-start | bytes 995336 | tf_op jit(solution)/shard_map/ppermute | solution.py:395
  28.4 1.0 %copy-start.4 = (f32[640,128]{1,0:T(8,128)S(1)}, f32[640,128]{1,0:T(8,128)}, u32[]{:S(2)}) copy-start(f32[640,128]{1,0:T(8,128)} %copy-done.3) | copy-start | bytes 983044
  32.6 11.4 %collective-permute-start.47 = (f32[640,128]{1,0:T(8,128)S(1)}, f32[640,128]{1,0:T(8,128)}, u32[]{:S(2)}, u32[]{:S(2)}) collective-permute-start(f32[640,128]{1,0:T(8,128)S(1)} %get-tuple-element.231.refs_1_), channel_id=1, source_target_pairs={{0,1},{1,0},{2,3},{3,2},{4,5},{5,4},{6,7},{7,6},{8,9},{9,8},{10,11... | collective-permute-start | bytes 983048 | tf_op jit(solution)/shard_map/ppermute | solution.py:395
  33.4 6.0 %collective-permute-start.34 = (f32[264,128]{1,0:T(8,128)S(1)}, f32[264,128]{1,0:T(8,128)}, u32[]{:S(2)}, u32[]{:S(2)}) collective-permute-start(f32[264,128]{1,0:T(8,128)S(1)} %param.34), channel_id=1, source_target_pairs={{0,10},{2,8},{4,14},{6,12},{8,2},{10,0},{12,6},{14,4},{16,26},{18,... | collective-permute-start | bytes 405512 | tf_op jit(solution)/shard_map/cond/branch_4_fun/ppermute | solution.py:395
  39.4 1.0 %copy-start.2 = (f32[640,128]{1,0:T(8,128)S(1)}, f32[640,128]{1,0:T(8,128)}, u32[]{:S(2)}) copy-start(f32[640,128]{1,0:T(8,128)} %copy-done.1) | copy-start | bytes 983044
  42.2 15.2 %collective-permute-start.50 = (f32[648,128]{1,0:T(8,128)S(1)}, f32[648,128]{1,0:T(8,128)S(1)}, u32[]{:S(2)}, u32[]{:S(2)}) collective-permute-start(f32[648,128]{1,0:T(8,128)S(1)} %get-tuple-element.243.refs_0_), channel_id=1, source_target_pairs={{0,1},{1,0},{2,3},{3,2},{4,5},{5,4},{6,7},{7,6},{8,9},{9,8},{10,11... | collective-permute-start | bytes 995336 | tf_op jit(solution)/shard_map/ppermute | solution.py:395
  46.6 12.5 %collective-permute-start.49 = (f32[640,128]{1,0:T(8,128)S(1)}, f32[640,128]{1,0:T(8,128)S(1)}, u32[]{:S(2)}, u32[]{:S(2)}) collective-permute-start(f32[640,128]{1,0:T(8,128)S(1)} %get-tuple-element.241.refs_0_), channel_id=1, source_target_pairs={{0,1},{1,0},{2,3},{3,2},{4,5},{5,4},{6,7},{7,6},{8,9},{9,8},{10,11... | collective-permute-start | bytes 983048 | tf_op jit(solution)/shard_map/ppermute | solution.py:395
  48.0 8.2 %collective-permute-start.51 = (f32[264,128]{1,0:T(8,128)S(1)}, f32[264,128]{1,0:T(8,128)S(1)}, u32[]{:S(2)}, u32[]{:S(2)}) collective-permute-start(f32[264,128]{1,0:T(8,128)S(1)} %get-tuple-element.247), channel_id=1, source_target_pairs={{0,30},{2,28},{4,26},{6,24},{8,22},{10,20},{12,18},{14,16},{16,14}... | collective-permute-start | bytes 405512 | tf_op jit(solution)/shard_map/ppermute | solution.py:395
where the time goes:
time: 60.4 us; the launch traced here: 60.5 us
  Pallas kernels  20.3 us (34%)
  waiting for transfers between devices  17.2 us (28%)
  starting transfers between devices  16.6 us (27%)
  local copies, waits for them, and re-layouts  3.46 us (6%)
  between operations  2.88 us (5%)
    ppermute x10, waiting for transfers between devices, swapped(): lax.ppermute(value, axis, [(a, a ^ mask) for a in range(lax.axis_size(axi...  17.2 us
    ppermute x10, starting transfers between devices, swapped(): lax.ppermute(value, axis, [(a, a ^ mask) for a in range(lax.axis_size(axi...  16.6 us
    pallas_call x6, Pallas kernels, stratum_call(): pl.pallas_call(kernel, out_shape=[jax.ShapeDtypeStruct(*spec) for spec in...  13.5 us
    unnamed x16, local copies, waits for them, and re-layouts  3.46 us
    pallas_call x2, Pallas kernels, user_log_call(): pl.pallas_call(functools.partial(user_log_kernel, at=at, rows=rows, facto...  2.55 us
    pallas_call x1, Pallas kernels, start_call(): pl.pallas_call(start_kernel, out_shape=[jax.ShapeDtypeStruct((rows, depth...  1.98 us
  transfers between devices with their start and end apart: 10, of which 4 were waited for; matrix products, arithmetic and copies ran while one was open for 0% of the time, Pallas kernels for 27%

commit v1 on v0

--- a/solution.py
+++ b/solution.py
@@ -103,8 +103,25 @@
 PARAMS = pltpu.CompilerParams(vmem_limit_bytes=24 * 2**20)
 
 
-def prepare_kernel(matchings, item_shape, item, *choices, last):
-    item[...] = item_shape[...].astype(F32)
+def in_hbm(x):
+    return pltpu.with_memory_space_constraint(x, pltpu.HBM)
+
+
+def in_vmem(x):
+    return pltpu.with_memory_space_constraint(x, pltpu.VMEM)
+
+
+def prepare_kernel(matchings_hbm, shape_hbm, item, *refs, last):
+    choices, (matchings, shape, sems) = refs[:STRATA], refs[STRATA:]
+    copies = [
+        pltpu.make_async_copy(shape_hbm, shape, sems.at[0]),
+        pltpu.make_async_copy(matchings_hbm, matchings, sems.at[1]),
+    ]
+    for copy in copies:
+        copy.start()
+    for copy in copies:
+        copy.wait()
+    item[...] = shape[...].astype(F32)
     choices[0][0] = matchings[0] - 1
     for stratum in range(1, STRATA - 1):
         choices[stratum][0] = jnp.bitwise_xor(matchings[stratum - 1], matchings[stratum]) - 1
@@ -116,11 +133,13 @@
         functools.partial(prepare_kernel, last=last),
         out_shape=[jax.ShapeDtypeStruct(item_shape.shape, F32)]
         + [jax.ShapeDtypeStruct((1,), jnp.int32)] * STRATA,
-        in_specs=[SMEM_SPEC, VMEM_SPEC],
+        in_specs=[HBM_SPEC, HBM_SPEC],
         out_specs=[VMEM_SPEC] + [SMEM_SPEC] * STRATA,
+        scratch_shapes=[pltpu.SMEM(matchings.shape, jnp.int32), pltpu.VMEM(item_shape.shape, BF16),
+                        pltpu.SemaphoreType.DMA((2,))],
         compiler_params=PARAMS,
         name="prepare",
-    )(matchings, item_shape)
+    )(in_hbm(matchings), in_hbm(item_shape))
     return out[0], [choice[0] for choice in out[1:]]
 
 
@@ -158,7 +177,7 @@
         cost_estimate=pl.CostEstimate(
             flops=40 * rows * depth, bytes_accessed=rows * depth * 4, transcendentals=2 * rows * depth),
         name="user_start",
-    )(user_shape)
+    )(in_hbm(user_shape))
 
 
 def stratum_kernel(names, *refs, stratum, at, rows, items, factor, first, last):
@@ -171,14 +190,11 @@
         copies[name].start()
 
     place = pl.ds(at, rows)
-    if first or last:
+    if first:
         fetch("item", ref["item"], ref["item_in"])
-    if stratum == 0:
-        fetch("uexp", ref["uexp_all"].at[place, :], ref["uexp"])
-    if stratum == 1:
-        fetch("shape", ref["user_shape"].at[place, :], ref["shape_in"])
     fetch("counts", ref["interactions"].at[stratum, place, :], ref["counts"])
-    upart, uexp, counts, ratios = ref["upart"], ref["uexp"], ref["counts"], ref["ratios"]
+    upart, counts, ratios, denominator = ref["upart"], ref["counts"], ref["ratios"], ref["denominator"]
+    uexp = ref["uexp_all"].at[place, :] if stratum == 0 else ref["uexp"]
     extra = 8 if first else 0
 
     def wait(name, general):
@@ -197,10 +213,8 @@
             else:
                 rte = ref["rte"][...]
             lows.append(rte)
-            if stratum == 1:
-                wait("shape", general)
             for t, step in tiles(rows):
-                old = ref["shape_in"][t:t + step, :].astype(F32) if stratum == 1 else ref["shp_old"][t:t + step, :]
+                old = ref["user_shape"][at + t:at + t + step, :].astype(F32) if stratum == 1 else ref["shp_old"][t:t + step, :]
                 stat = ref["acc"][extra + t:extra + t + step, :] + ref["recv"][extra + t:extra + t + step, :]
                 shp = 0.5 * old + 0.5 * (0.3 + factor * stat)
                 ref["shp_new"][t:t + step, :] = shp
@@ -213,9 +227,14 @@
         elif last:
             theta = ref["theta"][...]
 
-        if first or last:
+        if first:
             wait("item", general)
             item = ref["item_in"]
+            if not last:
+                ref["item_kept"][...] = item[...]
+        elif last:
+            item = ref["item_kept"]
+        if first or last:
             item_rte = None if stratum == 0 else item[items:items + 8, :]
         if first:
             value, sums, low = exp_tile(item[0:items, :], item_rte, general)
@@ -228,16 +247,14 @@
         else:
             item_exp = ref["item_exp"][...]
 
-        if stratum == 0:
-            wait("uexp", general)
+        denominator[...] = lax.dot_general(
+            uexp[...], item_exp, (((1,), (1,)), ((), ())), preferred_element_type=F32)
         wait("counts", general)
         for t, step in tiles(rows):
-            u = uexp[t:t + step, :]
-            denominator = lax.dot_general(u, item_exp, (((1,), (1,)), ((), ())), preferred_element_type=F32)
-            ratio = (counts[t:t + step, :].astype(F32) / denominator).astype(BF16)
-            ratios[t:t + step, :] = ratio
-            upart[extra + t:extra + t + step, :] = u.astype(F32) * jnp.dot(
-                ratio, item_exp, preferred_element_type=F32)
+            ratios[t:t + step, :] = (
+                counts[t:t + step, :].astype(F32) / denominator[t:t + step, :]).astype(BF16)
+        upart[extra:extra + rows, :] = uexp[...].astype(F32) * jnp.dot(
+            ratios[...], item_exp, preferred_element_type=F32)
         istat = lax.dot_general(ratios[...], uexp[...], (((0,), (0,)), ((), ())), preferred_element_type=F32)
         if not first:
             istat = istat + ref["istat"][...]
@@ -269,6 +286,8 @@
         outs["rte_new"] = ((8, depth), F32)
     if first:
         outs["item_exp_new"] = ((items, depth), BF16)
+    if first and not last:
+        outs["item_kept"] = (operands["item"].shape, F32)
     if last:
         outs["item_new"] = ((items + 8, depth), F32)
     else:
@@ -278,14 +297,17 @@
     scratch = {
         "counts": pltpu.VMEM((rows, items), BF16),
         "ratios": pltpu.VMEM((rows, items), BF16),
-        "uexp": pltpu.VMEM((rows, depth), BF16),
-        "sems": pltpu.SemaphoreType.DMA((3,)),
+        "denominator": pltpu.VMEM((rows, items), F32),
+        "sems": pltpu.SemaphoreType.DMA((2,)),
     }
-    if stratum == 1:
-        scratch["shape_in"] = pltpu.VMEM((rows, depth), BF16)
-    if first or last:
+    if stratum > 0:
+        scratch["uexp"] = pltpu.VMEM((rows, depth), BF16)
+    if first:
         scratch["item_in"] = pltpu.VMEM(operands["item"].shape, F32)
-    in_hbm = ("interactions", "user_shape", "uexp_all", "item")
+    hbm = ("interactions", "item")
+    operands = {
+        name: in_hbm(x) if name in hbm else in_vmem(x) if name == "user_shape" else x
+        for name, x in operands.items()}
     names = list(operands) + list(outs) + list(scratch)
     kernel = functools.partial(
         stratum_kernel, names, stratum=stratum, at=at, rows=rows, items=items,
@@ -293,7 +315,7 @@
     results = pl.pallas_call(
         kernel,
         out_shape=[jax.ShapeDtypeStruct(*spec) for spec in outs.values()],
-        in_specs=[HBM_SPEC if name in in_hbm else VMEM_SPEC for name in operands],
+        in_specs=[HBM_SPEC if name in hbm else VMEM_SPEC for name in operands],
         out_specs=[VMEM_SPEC] * len(outs),
         scratch_shapes=list(scratch.values()),
         compiler_params=PARAMS,
@@ -364,7 +386,7 @@
     )(*operands)
 
 
-def item_log_kernel(item, out, *, items):
+def item_log_kernel(item, _, out, *, items):
     rte = item[items:items + 8, :]
 
     def body(general):
@@ -378,17 +400,17 @@
         body(True)
 
 
-def item_log_call(item, items, depth):
+def item_log_call(item, after, items, depth):
     return pl.pallas_call(
         functools.partial(item_log_kernel, items=items),
         out_shape=jax.ShapeDtypeStruct((items, depth), BF16),
-        in_specs=[VMEM_SPEC],
+        in_specs=[VMEM_SPEC, VMEM_SPEC],
         out_specs=VMEM_SPEC,
         compiler_params=PARAMS,
         cost_estimate=pl.CostEstimate(
             flops=40 * items * depth, bytes_accessed=items * depth * 6, transcendentals=items * depth),
         name="item_log",
-    )(item)
+    )(item, after)
 
 
 def swapped(value, axis, mask):
@@ -446,8 +468,10 @@
                     operands["rte"] = rte
                 elif stratum > 1:
                     operands["rte_old"] = rte
-            if first or last:
+            if first:
                 operands["item"] = item
+            elif last:
+                operands["item_kept"] = carried["item_kept"]
             if not first:
                 operands["item_exp"] = carried["item_exp"]
                 operands["istat"] = carried["istat"]
@@ -459,6 +483,7 @@
             if first:
                 rte = out.get("rte_new")
                 carried["item_exp"] = out["item_exp_new"]
+                carried["item_kept"] = out.get("item_kept")
             if last:
                 item = out["item_new"]
             else:
@@ -469,13 +494,13 @@
             item, = moved(choices[stratum + 1], item)
         else:
             item = swapped(item, "users", group - 1)
-    item_log = item_log_call(item, items, depth)
     user_log = None
     for i, (at, rows) in enumerate(zip(starts, sizes)):
         out = user_log_call(at, rows, users, depth, factor, i == 0, (*sums[i], shp[i], rte), user_log)
         user_log = out[0]
         if i == 0:
             rte = out[1]
+            item_log = item_log_call(item, rte, items, depth)
     return user_log, item_log
 
 

time: 60.4 us -> 60.5 us (level)
  waiting for transfers between devices: 17.2 us -> 27 us
  Pallas kernels: 20.3 us -> 16.8 us
  local copies, waits for them, and re-layouts: 3.46 us -> 0.01 us
  starting transfers between devices: 16.6 us -> 13.9 us
    ppermute x10, waiting for transfers between devices: 17.2 us -> 27 us  [swapped(): lax.ppermute(value, axis, [(a, a ^ mask) for a in range(lax.axis_size(axi...]
    pallas_call x6, Pallas kernels: 13.5 us -> 9.83 us  [stratum_call(): pl.pallas_call(kernel, out_shape=[jax.ShapeDtypeStruct(*spec) for spec in...]
    unnamed x16 -> x2, local copies, waits for them, and re-layouts: 3.46 us -> 0.01 us
    ppermute x10, starting transfers between devices: 16.6 us -> 13.9 us  [swapped(): lax.ppermute(value, axis, [(a, a ^ mask) for a in range(lax.axis_size(axi...]
  transfers between devices with their start and end apart: 10 -> 10, of which waited for: 4 -> 7; matrix products, arithmetic and copies ran while one was open for 0% -> 0% of each run, Pallas kernels for 27% -> 20%
where the time goes in v1:
time: 60.5 us; the launch traced here: 60.7 us
  waiting for transfers between devices  27 us (45%)
  Pallas kernels  16.8 us (28%)
  starting transfers between devices  13.9 us (23%)
  between operations  2.83 us (5%)
    ppermute x10, waiting for transfers between devices, swapped(): lax.ppermute(value, axis, [(a, a ^ mask) for a in range(lax.axis_size(axi...  27 us
    ppermute x10, starting transfers between devices, swapped(): lax.ppermute(value, axis, [(a, a ^ mask) for a in range(lax.axis_size(axi...  13.9 us
    pallas_call x6, Pallas kernels, stratum_call(): pl.pallas_call(kernel, out_shape=[jax.ShapeDtypeStruct(*spec) for spec in...  9.83 us
    pallas_call x2, Pallas kernels, user_log_call(): pl.pallas_call(functools.partial(user_log_kernel, at=at, rows=rows, facto...  2.75 us
    pallas_call x1, Pallas kernels, start_call(): pl.pallas_call(start_kernel, out_shape=[jax.ShapeDtypeStruct((rows, depth...  1.94 us
    pallas_call x1, Pallas kernels, prepare_call(): pl.pallas_call(functools.partial(prepare_kernel, last=last), out_shape=[j...  1.4 us
  transfers between devices with their start and end apart: 10, of which 7 were waited for; matrix products, arithmetic and copies ran while one was open for 0% of the time, Pallas kernels for 20%

profile of v1, /device:TPU:0, one launch (start us, length us, event | category | flops | bytes accessed | tf_op | source)
XLA Modules:
  0.0 60.7 jit_solution(9426641336877366392)
XLA Ops:
  0.6 1.4 %prepare.1 = (f32[256,128]{1,0:T(8,128)S(1)}, s32[1]{0:T(128)}, s32[1]{0:T(128)}, s32[1]{0:T(128)}) custom-call(s32[3]{0:T(128)} %matchings_hbm.1, bf16[256,128]{1,0:T(8,128)(2,1)} %shape_hbm.1), custom_call_target="tpu_custom_call" | custom-call | tf_op jit(solution)/shard_map/prepare/pallas_call | solution.py:132
  2.7 6.7 %conditional.3 = (f32[256,128]{1,0:T(8,128)}, bf16[1280,128]{1,0:T(8,128)(2,1)S(1)}, f32[8,128]{1,0:T(8,128)S(1)}) conditional(s32[]{:T(128)} %bitcast, (f32[256,128]{1,0:T(8,128)S(1)}, bf16[1280,128]{1,0:T(8,128)(2,1)}) %tuple.158, (f32[256,128]{1,0:T(8,128)S(1)}, bf16[1280,128]{1,0:T(8,128)(2,1)}) %tuple.158, ...), branch_computations={%region_0.0_spmd, %region_1.0_spmd, %region_2.0_spmd, %region_3.0_... | conditional | flops 6553600 | bytes 1179712 | solution.py:426
  2.7 3.1 %collective-permute-start.3 = (f32[256,128]{1,0:T(8,128)S(1)}, f32[256,128]{1,0:T(8,128)}, u32[]{:S(2)}, u32[]{:S(2)}) collective-permute-start(f32[256,128]{1,0:T(8,128)S(1)} %get-tuple-element.134), channel_id=1, source_target_pairs={{0,8},{2,10},{4,12},{6,14},{8,0},{10,2},{12,4},{14,6},{16,24},{18,... | collective-permute-start | bytes 393224 | tf_op jit(solution)/shard_map/cond/branch_3_fun/ppermute | solution.py:417
  5.8 1.9 %user_start.18 = (bf16[1280,128]{1,0:T(8,128)(2,1)S(1)}, f32[8,128]{1,0:T(8,128)S(1)}) custom-call(bf16[1280,128]{1,0:T(8,128)(2,1)} %get-tuple-element.135.shape), custom_call_target="tpu_custom_call" | custom-call | flops 6553600 | bytes 655360 | tf_op jit(solution)/shard_map/cond/branch_3_fun/user_start/pallas_call | solution.py:171
  7.8 1.7 %collective-permute-done.3 = f32[256,128]{1,0:T(8,128)} collective-permute-done((f32[256,128]{1,0:T(8,128)S(1)}, f32[256,128]{1,0:T(8,128)}, u32[]{:S(2)}, u32[]{:S(2)}) %collective-permute-start.3) | collective-permute-done | bytes 131104 | tf_op jit(solution)/shard_map/cond/branch_3_fun/ppermute | solution.py:417
  9.4 0.0 copy-start
  9.4 1.8 %stratum0_at0.1 = (f32[648,128]{1,0:T(8,128)S(1)}, bf16[256,128]{1,0:T(8,128)(2,1)S(1)}, f32[256,128]{1,0:T(8,128)S(1)}, f32[256,128]{1,0:T(8,128)S(1)}) custom-call(bf16[3,1280,256]{2,1,0:T(8,128)(2,1)} %refs_0_.11, bf16[1280,128]{1,0:T(8,128)(2,1)S(1)} %get-tuple-element.221.refs_1_, f32[256,128]{1,0:T(8,128)} %get-tuple-element.222.refs_2_), custom_call_target="tpu_custom_call" | custom-call | flops 125829120 | bytes 1638400 | tf_op jit(solution)/shard_map/stratum0_at0/pallas_call | solution.py:315
  11.3 1.7 %collective-permute-start.46 = (f32[648,128]{1,0:T(8,128)S(1)}, f32[648,128]{1,0:T(8,128)S(1)}, u32[]{:S(2)}, u32[]{:S(2)}) collective-permute-start(f32[648,128]{1,0:T(8,128)S(1)} %get-tuple-element.228.refs_1_), channel_id=1, source_target_pairs={{0,1},{1,0},{2,3},{3,2},{4,5},{5,4},{6,7},{7,6},{8,9},{9,8},{10,11... | collective-permute-start | bytes 995336 | tf_op jit(solution)/shard_map/ppermute | solution.py:417
  13.0 1.4 %stratum0_at640.1 = (f32[640,128]{1,0:T(8,128)S(1)}, f32[264,128]{1,0:T(8,128)S(1)}) custom-call(bf16[3,1280,256]{2,1,0:T(8,128)(2,1)} %refs_0_.11, bf16[1280,128]{1,0:T(8,128)(2,1)S(1)} %get-tuple-element.221.refs_1_, f32[256,128]{1,0:T(8,128)S(1)} %get-tuple-element.223.refs_2_, bf16[256,128]{1,0:T(8,128)(2,1)S(1)} %get-tuple-element.224.refs_3_, ...), custom_call_target="tpu_custom_call" | custom-call | flops 125829120 | bytes 1638400 | tf_op jit(solution)/shard_map/stratum0_at640/pallas_call | solution.py:315
  14.4 0.4 collective-permute-start.45
  15.5 6.1 %conditional.4 = (f32[264,128]{1,0:T(8,128)}) conditional(s32[]{:T(128)} %bitcast.1, f32[264,128]{1,0:T(8,128)S(1)} %get-tuple-element.230, f32[264,128]{1,0:T(8,128)S(1)} %get-tuple-element.230, f32[264,128]{1,0:T(8,128)S(1)} %get-tuple-element.230, f32[264,128]{1,0:T(8,128)S(1)} %get-tuple-element.230, ...), branch_computations={%region_15.0_spmd, %region_16.0_spmd, %region_17.0_spmd, %region_1... | conditional | bytes 540720 | solution.py:426
  15.5 2.8 %collective-permute-start.20 = (f32[264,128]{1,0:T(8,128)S(1)}, f32[264,128]{1,0:T(8,128)}, u32[]{:S(2)}, u32[]{:S(2)}) collective-permute-start(f32[264,128]{1,0:T(8,128)S(1)} %param.20), channel_id=1, source_target_pairs={{0,12},{2,14},{4,8},{6,10},{8,4},{10,6},{12,0},{14,2},{16,28},{18,... | collective-permute-start | bytes 405512 | tf_op jit(solution)/shard_map/cond/branch_5_fun/ppermute | solution.py:417
  18.3 3.3 %collective-permute-done.20 = f32[264,128]{1,0:T(8,128)} collective-permute-done((f32[264,128]{1,0:T(8,128)S(1)}, f32[264,128]{1,0:T(8,128)}, u32[]{:S(2)}, u32[]{:S(2)}) %collective-permute-start.20) | collective-permute-done | bytes 135200 | tf_op jit(solution)/shard_map/cond/branch_5_fun/ppermute | solution.py:417
  21.6 0.5 collective-permute-done.46.refs_2_
  22.1 0.0 copy-done
  22.1 2.0 %stratum1_at0.1 = (f32[648,128]{1,0:T(8,128)S(1)}, f32[640,128]{1,0:T(8,128)S(1)}, f32[8,128]{1,0:T(8,128)S(1)}, bf16[256,128]{1,0:T(8,128)(2,1)S(1)}, f32[264,1...) custom-call(bf16[3,1280,256]{2,1,0:T(8,128)(2,1)} %refs_0_.11, ...), custom_call_target="tpu_custom_call" | custom-call | flops 125829120 | bytes 1638400 | tf_op jit(solution)/shard_map/stratum1_at0/pallas_call | solution.py:315
  24.0 1.7 %collective-permute-start.48 = (f32[648,128]{1,0:T(8,128)S(1)}, f32[648,128]{1,0:T(8,128)S(1)}, u32[]{:S(2)}, u32[]{:S(2)}) collective-permute-start(f32[648,128]{1,0:T(8,128)S(1)} %get-tuple-element.238.refs_1_), channel_id=1, source_target_pairs={{0,1},{1,0},{2,3},{3,2},{4,5},{5,4},{6,7},{7,6},{8,9},{9,8},{10,11... | collective-permute-start | bytes 995336 | tf_op jit(solution)/shard_map/ppermute | solution.py:417
  25.8 3.3 %collective-permute-done.45.refs_2_ = f32[640,128]{1,0:T(8,128)S(1)} collective-permute-done((f32[640,128]{1,0:T(8,128)S(1)}, f32[640,128]{1,0:T(8,128)S(1)}, u32[]{:S(2)}, u32[]{:S(2)}) %collective-permute-start.45) | collective-permute-done | bytes 327712 | tf_op jit(solution)/shard_map/ppermute | solution.py:417
  29.1 1.4 %stratum1_at640.1 = (f32[640,128]{1,0:T(8,128)S(1)}, f32[640,128]{1,0:T(8,128)S(1)}, f32[264,128]{1,0:T(8,128)S(1)}) custom-call(bf16[3,1280,256]{2,1,0:T(8,128)(2,1)} %refs_0_.11, f32[640,128]{1,0:T(8,128)S(1)} %get-tuple-element.227.refs_1_, f32[640,128]{1,0:T(8,128)S(1)} %collective-permute-done.45.refs_2_, bf16[1280,128]{1,0:T(8,128)(2,1)S(1)} %copy-done, ...), custom_call_target="tpu_custom_call" | custom-call | flops 125829120 | bytes 1638400 | tf_op jit(solution)/shard_map/stratum1_at640/pallas_call | solution.py:315
  30.5 1.7 %collective-permute-start.47 = (f32[640,128]{1,0:T(8,128)S(1)}, f32[640,128]{1,0:T(8,128)S(1)}, u32[]{:S(2)}, u32[]{:S(2)}) collective-permute-start(f32[640,128]{1,0:T(8,128)S(1)} %get-tuple-element.236.refs_1_), channel_id=1, source_target_pairs={{0,1},{1,0},{2,3},{3,2},{4,5},{5,4},{6,7},{7,6},{8,9},{9,8},{10,11... | collective-permute-start | bytes 983048 | tf_op jit(solution)/shard_map/ppermute | solution.py:417
  32.9 7.7 %conditional.5 = (f32[264,128]{1,0:T(8,128)}) conditional(s32[]{:T(128)} %bitcast.2, f32[264,128]{1,0:T(8,128)S(1)} %get-tuple-element.241, f32[264,128]{1,0:T(8,128)S(1)} %get-tuple-element.241, f32[264,128]{1,0:T(8,128)S(1)} %get-tuple-element.241, f32[264,128]{1,0:T(8,128)S(1)} %get-tuple-element.241, ...), branch_computations={%region_30.0_spmd, %region_31.0_spmd, %region_32.0_spmd, %region_3... | conditional | bytes 540720 | solution.py:426
  32.9 0.1 collective-permute-start.42
  33.0 7.6 %collective-permute-done.42 = f32[264,128]{1,0:T(8,128)} collective-permute-done((f32[264,128]{1,0:T(8,128)S(1)}, f32[264,128]{1,0:T(8,128)}, u32[]{:S(2)}, u32[]{:S(2)}) %collective-permute-start.42) | collective-permute-done | bytes 135200 | tf_op jit(solution)/shard_map/cond/branch_12_fun/ppermute | solution.py:417
  40.6 0.0 collective-permute-done.48.refs_2_
  40.6 1.8 %stratum2_at0.1 = (f32[648,128]{1,0:T(8,128)S(1)}, f32[640,128]{1,0:T(8,128)S(1)}, f32[8,128]{1,0:T(8,128)S(1)}, bf16[256,128]{1,0:T(8,128)(2,1)S(1)}, f32[264,1...) custom-call(bf16[3,1280,256]{2,1,0:T(8,128)(2,1)} %refs_0_.11, ...), custom_call_target="tpu_custom_call" | custom-call | flops 125829120 | bytes 1638400 | tf_op jit(solution)/shard_map/stratum2_at0/pallas_call | solution.py:315
  42.4 0.3 collective-permute-start.50
  42.6 0.0 collective-permute-done.47.refs_2_
  42.6 1.4 %stratum2_at640.1 = (f32[640,128]{1,0:T(8,128)S(1)}, f32[640,128]{1,0:T(8,128)S(1)}, f32[264,128]{1,0:T(8,128)S(1)}) custom-call(bf16[3,1280,256]{2,1,0:T(8,128)(2,1)} %refs_0_.11, f32[640,128]{1,0:T(8,128)S(1)} %get-tuple-element.236.refs_1_, f32[640,128]{1,0:T(8,128)S(1)} %collective-permute-done.47.refs_2_, f32[640,128]{1,0:T(8,128)S(1)} %get-tuple-element.237.refs_3_, ...), custom_call_target="tpu_custom_call" | custom-call | flops 125829120 | bytes 1638400 | tf_op jit(solution)/shard_map/stratum2_at640/pallas_call | solution.py:315
  44.1 1.9 %collective-permute-start.49 = (f32[640,128]{1,0:T(8,128)S(1)}, f32[640,128]{1,0:T(8,128)S(1)}, u32[]{:S(2)}, u32[]{:S(2)}) collective-permute-start(f32[640,128]{1,0:T(8,128)S(1)} %get-tuple-element.247.refs_0_), channel_id=1, source_target_pairs={{0,1},{1,0},{2,3},{3,2},{4,5},{5,4},{6,7},{7,6},{8,9},{9,8},{10,11... | collective-permute-start | bytes 983048 | tf_op jit(solution)/shard_map/ppermute | solution.py:417
  46.0 0.2 collective-permute-start.51
  46.2 6.9 %collective-permute-done.50.refs_1_ = f32[648,128]{1,0:T(8,128)S(1)} collective-permute-done((f32[648,128]{1,0:T(8,128)S(1)}, f32[648,128]{1,0:T(8,128)S(1)}, u32[]{:S(2)}, u32[]{:S(2)}) %collective-permute-start.50) | collective-permute-done | bytes 331808 | tf_op jit(solution)/shard_map/ppermute | solution.py:417
  53.1 1.5 %user_log_at0.1 = (bf16[1280,128]{1,0:T(8,128)(2,1)}, f32[8,128]{1,0:T(8,128)S(1)}) custom-call(f32[648,128]{1,0:T(8,128)S(1)} %get-tuple-element.249.refs_0_, f32[648,128]{1,0:T(8,128)S(1)} %collective-permute-done.50.refs_1_, f32[640,128]{1,0:T(8,128)S(1)} %get-tuple-element.250.refs_2_, f32[8,128]{1,0:T(8,128)S(1)} %get-tuple-element.242.refs_4_.refs_3_), custom_call_target="tpu_custom_call" | custom-call | flops 3276800 | bytes 1146880 | tf_op jit(solution)/shard_map/user_log_at0/pallas_call | solution.py:374
  54.6 0.0 collective-permute-done.51.item
  54.6 0.9 %item_log.1 = bf16[256,128]{1,0:T(8,128)(2,1)} custom-call(f32[264,128]{1,0:T(8,128)S(1)} %collective-permute-done.51.item, f32[8,128]{1,0:T(8,128)S(1)} %get-tuple-element.251.refs_3_._), custom_call_target="tpu_custom_call" | custom-call | flops 1310720 | bytes 196608 | tf_op jit(solution)/shard_map/item_log/pallas_call | solution.py:404
  55.6 3.7 %collective-permute-done.49.refs_1_ = f32[640,128]{1,0:T(8,128)S(1)} collective-permute-done((f32[640,128]{1,0:T(8,128)S(1)}, f32[640,128]{1,0:T(8,128)S(1)}, u32[]{:S(2)}, u32[]{:S(2)}) %collective-permute-start.49) | collective-permute-done | bytes 327712 | tf_op jit(solution)/shard_map/ppermute | solution.py:417
  59.3 1.3 %user_log_at640.1 = bf16[1280,128]{1,0:T(8,128)(2,1)} custom-call(f32[640,128]{1,0:T(8,128)S(1)} %get-tuple-element.247.refs_0_, f32[640,128]{1,0:T(8,128)S(1)} %collective-permute-done.49.refs_1_, f32[640,128]{1,0:T(8,128)S(1)} %get-tuple-element.248.refs_2_, f32[8,128]{1,0:T(8,128)S(1)} %get-tuple-element.251.refs_3_._, ...), custom_call_target="tpu_custom_call", output_to_operand_aliasing={{}: (4, {})} | custom-call | flops 3276800 | bytes 1146880 | tf_op jit(solution)/shard_map/user_log_at640/pallas_call | solution.py:374
Async XLA Ops:
  2.7 6.7 %collective-permute-start.3 = (f32[256,128]{1,0:T(8,128)S(1)}, f32[256,128]{1,0:T(8,128)}, u32[]{:S(2)}, u32[]{:S(2)}) collective-permute-start(f32[256,128]{1,0:T(8,128)S(1)} %get-tuple-element.134), channel_id=1, source_target_pairs={{0,8},{2,10},{4,12},{6,14},{8,0},{10,2},{12,4},{14,6},{16,24},{18,... | collective-permute-start | bytes 393224 | tf_op jit(solution)/shard_map/cond/branch_3_fun/ppermute | solution.py:417
  9.4 12.6 %copy-start = (bf16[1280,128]{1,0:T(8,128)(2,1)S(1)}, bf16[1280,128]{1,0:T(8,128)(2,1)}, u32[]{:S(2)}) copy-start(bf16[1280,128]{1,0:T(8,128)(2,1)} %refs_3_.3) | copy-start | bytes 983044
  11.3 10.8 %collective-permute-start.46 = (f32[648,128]{1,0:T(8,128)S(1)}, f32[648,128]{1,0:T(8,128)S(1)}, u32[]{:S(2)}, u32[]{:S(2)}) collective-permute-start(f32[648,128]{1,0:T(8,128)S(1)} %get-tuple-element.228.refs_1_), channel_id=1, source_target_pairs={{0,1},{1,0},{2,3},{3,2},{4,5},{5,4},{6,7},{7,6},{8,9},{9,8},{10,11... | collective-permute-start | bytes 995336 | tf_op jit(solution)/shard_map/ppermute | solution.py:417
  14.4 14.7 %collective-permute-start.45 = (f32[640,128]{1,0:T(8,128)S(1)}, f32[640,128]{1,0:T(8,128)S(1)}, u32[]{:S(2)}, u32[]{:S(2)}) collective-permute-start(f32[640,128]{1,0:T(8,128)S(1)} %get-tuple-element.227.refs_1_), channel_id=1, source_target_pairs={{0,1},{1,0},{2,3},{3,2},{4,5},{5,4},{6,7},{7,6},{8,9},{9,8},{10,11... | collective-permute-start | bytes 983048 | tf_op jit(solution)/shard_map/ppermute | solution.py:417
  15.5 6.1 %collective-permute-start.20 = (f32[264,128]{1,0:T(8,128)S(1)}, f32[264,128]{1,0:T(8,128)}, u32[]{:S(2)}, u32[]{:S(2)}) collective-permute-start(f32[264,128]{1,0:T(8,128)S(1)} %param.20), channel_id=1, source_target_pairs={{0,12},{2,14},{4,8},{6,10},{8,4},{10,6},{12,0},{14,2},{16,28},{18,... | collective-permute-start | bytes 405512 | tf_op jit(solution)/shard_map/cond/branch_5_fun/ppermute | solution.py:417
  24.0 16.5 %collective-permute-start.48 = (f32[648,128]{1,0:T(8,128)S(1)}, f32[648,128]{1,0:T(8,128)S(1)}, u32[]{:S(2)}, u32[]{:S(2)}) collective-permute-start(f32[648,128]{1,0:T(8,128)S(1)} %get-tuple-element.238.refs_1_), channel_id=1, source_target_pairs={{0,1},{1,0},{2,3},{3,2},{4,5},{5,4},{6,7},{7,6},{8,9},{9,8},{10,11... | collective-permute-start | bytes 995336 | tf_op jit(solution)/shard_map/ppermute | solution.py:417
  30.5 12.1 %collective-permute-start.47 = (f32[640,128]{1,0:T(8,128)S(1)}, f32[640,128]{1,0:T(8,128)S(1)}, u32[]{:S(2)}, u32[]{:S(2)}) collective-permute-start(f32[640,128]{1,0:T(8,128)S(1)} %get-tuple-element.236.refs_1_), channel_id=1, source_target_pairs={{0,1},{1,0},{2,3},{3,2},{4,5},{5,4},{6,7},{7,6},{8,9},{9,8},{10,11... | collective-permute-start | bytes 983048 | tf_op jit(solution)/shard_map/ppermute | solution.py:417
  32.9 7.7 %collective-permute-start.42 = (f32[264,128]{1,0:T(8,128)S(1)}, f32[264,128]{1,0:T(8,128)}, u32[]{:S(2)}, u32[]{:S(2)}) collective-permute-start(f32[264,128]{1,0:T(8,128)S(1)} %param.42), channel_id=1, source_target_pairs={{0,26},{2,24},{4,30},{6,28},{8,18},{10,16},{12,22},{14,20},{16,10}... | collective-permute-start | bytes 405512 | tf_op jit(solution)/shard_map/cond/branch_12_fun/ppermute | solution.py:417
  42.4 10.7 %collective-permute-start.50 = (f32[648,128]{1,0:T(8,128)S(1)}, f32[648,128]{1,0:T(8,128)S(1)}, u32[]{:S(2)}, u32[]{:S(2)}) collective-permute-start(f32[648,128]{1,0:T(8,128)S(1)} %get-tuple-element.249.refs_0_), channel_id=1, source_target_pairs={{0,1},{1,0},{2,3},{3,2},{4,5},{5,4},{6,7},{7,6},{8,9},{9,8},{10,11... | collective-permute-start | bytes 995336 | tf_op jit(solution)/shard_map/ppermute | solution.py:417
  44.1 15.2 %collective-permute-start.49 = (f32[640,128]{1,0:T(8,128)S(1)}, f32[640,128]{1,0:T(8,128)S(1)}, u32[]{:S(2)}, u32[]{:S(2)}) collective-permute-start(f32[640,128]{1,0:T(8,128)S(1)} %get-tuple-element.247.refs_0_), channel_id=1, source_target_pairs={{0,1},{1,0},{2,3},{3,2},{4,5},{5,4},{6,7},{7,6},{8,9},{9,8},{10,11... | collective-permute-start | bytes 983048 | tf_op jit(solution)/shard_map/ppermute | solution.py:417
  46.0 8.7 %collective-permute-start.51 = (f32[264,128]{1,0:T(8,128)S(1)}, f32[264,128]{1,0:T(8,128)S(1)}, u32[]{:S(2)}, u32[]{:S(2)}) collective-permute-start(f32[264,128]{1,0:T(8,128)S(1)} %get-tuple-element.253), channel_id=1, source_target_pairs={{0,30},{2,28},{4,26},{6,24},{8,22},{10,20},{12,18},{14,16},{16,14}... | collective-permute-start | bytes 405512 | tf_op jit(solution)/shard_map/ppermute | solution.py:417

commit v2 on v1

--- a/solution.py
+++ b/solution.py
@@ -14,8 +14,12 @@
 
 
 def chunk_rows(rows):
-    half = rows // 2 // TILE * TILE
-    return [half, rows - half]
+    first = max(rows // 2 // TILE, 1) * TILE
+    return [first, rows - first] if first < rows else [rows]
+
+
+def tail_rows(rows):
+    return 2 * TILE if rows > 4 * TILE else 0
 
 
 def psi_parts(x):
@@ -132,7 +136,7 @@
     out = pl.pallas_call(
         functools.partial(prepare_kernel, last=last),
         out_shape=[jax.ShapeDtypeStruct(item_shape.shape, F32)]
-        + [jax.ShapeDtypeStruct((1,), jnp.int32)] * STRATA,
+        + [pltpu.SMEM((1,), jnp.int32)] * STRATA,
         in_specs=[HBM_SPEC, HBM_SPEC],
         out_specs=[VMEM_SPEC] + [SMEM_SPEC] * STRATA,
         scratch_shapes=[pltpu.SMEM(matchings.shape, jnp.int32), pltpu.VMEM(item_shape.shape, BF16),
@@ -180,7 +184,7 @@
     )(in_hbm(user_shape))
 
 
-def stratum_kernel(names, *refs, stratum, at, rows, items, factor, first, last):
+def stratum_kernel(names, *refs, stratum, at, rows, items, factor, first, last, tail):
     ref = dict(zip(names, refs))
     sems = ref["sems"]
     copies = {}
@@ -253,8 +257,11 @@
         for t, step in tiles(rows):
             ratios[t:t + step, :] = (
                 counts[t:t + step, :].astype(F32) / denominator[t:t + step, :]).astype(BF16)
-        upart[extra:extra + rows, :] = uexp[...].astype(F32) * jnp.dot(
+        user_sums = uexp[...].astype(F32) * jnp.dot(
             ratios[...], item_exp, preferred_element_type=F32)
+        upart[extra:extra + rows - tail, :] = user_sums[0:rows - tail, :]
+        if tail:
+            ref["upart_tail"][...] = user_sums[rows - tail:, :]
         istat = lax.dot_general(ratios[...], uexp[...], (((0,), (0,)), ((), ())), preferred_element_type=F32)
         if not first:
             istat = istat + ref["istat"][...]
@@ -277,9 +284,11 @@
             body(True)
 
 
-def stratum_call(stratum, at, rows, items, depth, factor, first, last, operands):
+def stratum_call(stratum, at, rows, items, depth, factor, first, last, tail, operands):
     extra = 8 if first else 0
-    outs = {"upart": ((rows + extra, depth), F32)}
+    outs = {"upart": ((rows + extra - tail, depth), F32)}
+    if tail:
+        outs["upart_tail"] = ((tail, depth), F32)
     if stratum > 0:
         outs["shp_new"] = ((rows, depth), F32)
     if first and stratum > 0:
@@ -311,7 +320,7 @@
     names = list(operands) + list(outs) + list(scratch)
     kernel = functools.partial(
         stratum_kernel, names, stratum=stratum, at=at, rows=rows, items=items,
-        factor=factor, first=first, last=last)
+        factor=factor, first=first, last=last, tail=tail)
     results = pl.pallas_call(
         kernel,
         out_shape=[jax.ShapeDtypeStruct(*spec) for spec in outs.values()],
@@ -319,15 +328,13 @@
         out_specs=[VMEM_SPEC] * len(outs),
         scratch_shapes=list(scratch.values()),
         compiler_params=PARAMS,
-        cost_estimate=pl.CostEstimate(
-            flops=6 * rows * items * depth, bytes_accessed=rows * (items * 2 + depth * 16),
-            transcendentals=rows * (depth + items)),
+        cost_estimate=pl.CostEstimate(flops=1, bytes_accessed=1, transcendentals=0),
         name=f"stratum{stratum}_at{at}",
     )(*operands.values())
     return dict(zip(outs, results))
 
 
-def user_log_kernel(*refs, at, rows, factor, first, filled):
+def user_log_kernel(*refs, at, rows, shp_at, factor, first, filled):
     acc, recv, shp_old, rte_in = refs[:4]
     rest = refs[5:] if filled else refs[4:]
     if first:
@@ -344,7 +351,7 @@
         low = rte
         for t, step in tiles(rows):
             stat = acc[extra + t:extra + t + step, :] + recv[extra + t:extra + t + step, :]
-            shp = 0.5 * shp_old[t:t + step, :] + 0.5 * (0.3 + factor * stat)
+            shp = 0.5 * shp_old[shp_at + t:shp_at + t + step, :] + 0.5 * (0.3 + factor * stat)
             block[t:t + step, :], part_low = log_tile(shp, rte, general)
             low = jnp.minimum(low, part_low)
         return low
@@ -360,7 +367,7 @@
     copy.wait()
 
 
-def user_log_call(at, rows, total, depth, factor, first, operands, filled):
+def user_log_call(at, rows, shp_at, total, depth, factor, first, operands, filled):
     out_shape = [jax.ShapeDtypeStruct((total, depth), BF16)]
     out_specs = [HBM_SPEC]
     if first:
@@ -372,7 +379,7 @@
         operands.append(filled)
         in_specs.append(HBM_SPEC)
     return pl.pallas_call(
-        functools.partial(user_log_kernel, at=at, rows=rows, factor=factor, first=first,
+        functools.partial(user_log_kernel, at=at, rows=rows, shp_at=shp_at, factor=factor, first=first,
                           filled=filled is not None),
         out_shape=out_shape,
         in_specs=in_specs,
@@ -477,9 +484,12 @@
                 operands["istat"] = carried["istat"]
             if (stratum > 0 and not first) or (stratum == 0 and last):
                 operands["theta"] = carried["theta"]
-            out = stratum_call(stratum, at, rows, items, depth, factor, first, last, operands)
+            tail = tail_rows(rows) if last and stratum == STRATA - 1 else 0
+            out = stratum_call(stratum, at, rows, items, depth, factor, first, last, tail, operands)
             shp[i] = out.get("shp_new")
             sums[i] = exchanged(out["upart"])
+            if tail:
+                tail_sums = exchanged(out["upart_tail"])
             if first:
                 rte = out.get("rte_new")
                 carried["item_exp"] = out["item_exp_new"]
@@ -495,8 +505,13 @@
         else:
             item = swapped(item, "users", group - 1)
     user_log = None
-    for i, (at, rows) in enumerate(zip(starts, sizes)):
-        out = user_log_call(at, rows, users, depth, factor, i == 0, (*sums[i], shp[i], rte), user_log)
+    pieces = [(at, rows, 0, sums[i], shp[i]) for i, (at, rows) in enumerate(zip(starts, sizes))]
+    if tail:
+        at, rows = starts[-1], sizes[-1] - tail
+        pieces[-1:] = [(at, rows, 0, sums[-1], shp[-1]), (at + rows, tail, rows, tail_sums, shp[-1])]
+    for i, (at, rows, shp_at, piece_sums, piece_shp) in enumerate(pieces):
+        out = user_log_call(
+            at, rows, shp_at, users, depth, factor, i == 0, (*piece_sums, piece_shp, rte), user_log)
         user_log = out[0]
         if i == 0:
             rte = out[1]

time: 60.5 us -> 56.9 us (0.940)
  waiting for transfers between devices: 27 us -> 22.9 us
  starting transfers between devices: 13.9 us -> 16.7 us
  between operations: 2.83 us -> 0.91 us
    ppermute x10 -> x11, waiting for transfers between devices: 27 us -> 22.9 us  [swapped(): lax.ppermute(value, axis, [(a, a ^ mask) for a in range(lax.axis_size(axi...]
    ppermute x10 -> x11, starting transfers between devices: 13.9 us -> 16.7 us  [swapped(): lax.ppermute(value, axis, [(a, a ^ mask) for a in range(lax.axis_size(axi...]
    pallas_call x2 -> x3, Pallas kernels: 2.75 us -> 3.51 us  [user_log_call(): pl.pallas_call(functools.partial(user_log_kernel, at=at, rows=rows, shp_a...]
  transfers between devices with their start and end apart: 10 -> 11, of which waited for: 7 -> 9; matrix products, arithmetic and copies ran while one was open for 0% -> 0% of each run, Pallas kernels for 20% -> 23%
where the time goes in v2:
time: 56.9 us; the launch traced here: 57.6 us
  waiting for transfers between devices  22.9 us (40%)
  Pallas kernels  17.1 us (30%)
  starting transfers between devices  16.7 us (29%)
  between operations  0.91 us (2%)
    ppermute x11, waiting for transfers between devices, swapped(): lax.ppermute(value, axis, [(a, a ^ mask) for a in range(lax.axis_size(axi...  22.9 us
    ppermute x11, starting transfers between devices, swapped(): lax.ppermute(value, axis, [(a, a ^ mask) for a in range(lax.axis_size(axi...  16.7 us
    pallas_call x6, Pallas kernels, stratum_call(): pl.pallas_call(kernel, out_shape=[jax.ShapeDtypeStruct(*spec) for spec in...  9.83 us
    pallas_call x3, Pallas kernels, user_log_call(): pl.pallas_call(functools.partial(user_log_kernel, at=at, rows=rows, shp_a...  3.51 us
    pallas_call x1, Pallas kernels, start_call(): pl.pallas_call(start_kernel, out_shape=[jax.ShapeDtypeStruct((rows, depth...  1.94 us
  transfers between devices with their start and end apart: 11, of which 9 were waited for; matrix products, arithmetic and copies ran while one was open for 0% of the time, Pallas kernels for 23%

profile of v2, /device:TPU:0, one launch (start us, length us, event | category | flops | bytes accessed | tf_op | source)
XLA Modules:
  0.0 57.6 jit_solution(7991506493901351654)
XLA Ops:
  0.6 0.9 %prepare.1 = (f32[256,128]{1,0:T(8,128)S(1)}, s32[1]{0:T(128)S(4)}, s32[1]{0:T(128)S(4)}, s32[1]{0:T(128)S(4)}) custom-call(s32[3]{0:T(128)} %matchings_hbm.1, bf16[256,128]{1,0:T(8,128)(2,1)} %shape_hbm.1), custom_call_target="tpu_custom_call" | custom-call | tf_op jit(solution)/shard_map/prepare/pallas_call | solution.py:136
  1.5 6.7 %conditional.3 = (f32[256,128]{1,0:T(8,128)}, bf16[1280,128]{1,0:T(8,128)(2,1)S(1)}, f32[8,128]{1,0:T(8,128)S(1)}) conditional(s32[]{:T(128)} %bitcast, (f32[256,128]{1,0:T(8,128)S(1)}, bf16[1280,128]{1,0:T(8,128)(2,1)}) %tuple.158, (f32[256,128]{1,0:T(8,128)S(1)}, bf16[1280,128]{1,0:T(8,128)(2,1)}) %tuple.158, ...), branch_computations={%region_0.0_spmd, %region_1.0_spmd, %region_2.0_spmd, %region_3.0_... | conditional | flops 6553600 | bytes 1179712 | solution.py:433
  1.6 3.1 %collective-permute-start.3 = (f32[256,128]{1,0:T(8,128)S(1)}, f32[256,128]{1,0:T(8,128)}, u32[]{:S(2)}, u32[]{:S(2)}) collective-permute-start(f32[256,128]{1,0:T(8,128)S(1)} %get-tuple-element.134), channel_id=1, source_target_pairs={{0,8},{2,10},{4,12},{6,14},{8,0},{10,2},{12,4},{14,6},{16,24},{18,... | collective-permute-start | bytes 393224 | tf_op jit(solution)/shard_map/cond/branch_3_fun/ppermute | solution.py:424
  4.6 1.9 %user_start.18 = (bf16[1280,128]{1,0:T(8,128)(2,1)S(1)}, f32[8,128]{1,0:T(8,128)S(1)}) custom-call(bf16[1280,128]{1,0:T(8,128)(2,1)} %get-tuple-element.135.shape), custom_call_target="tpu_custom_call" | custom-call | flops 6553600 | bytes 655360 | tf_op jit(solution)/shard_map/cond/branch_3_fun/user_start/pallas_call | solution.py:175
  6.6 1.7 %collective-permute-done.3 = f32[256,128]{1,0:T(8,128)} collective-permute-done((f32[256,128]{1,0:T(8,128)S(1)}, f32[256,128]{1,0:T(8,128)}, u32[]{:S(2)}, u32[]{:S(2)}) %collective-permute-start.3) | collective-permute-done | bytes 131104 | tf_op jit(solution)/shard_map/cond/branch_3_fun/ppermute | solution.py:424
  8.2 0.0 copy-start
  8.2 1.8 %stratum0_at0.1 = (f32[648,128]{1,0:T(8,128)S(1)}, bf16[256,128]{1,0:T(8,128)(2,1)S(1)}, f32[256,128]{1,0:T(8,128)S(1)}, f32[256,128]{1,0:T(8,128)S(1)}) custom-call(bf16[3,1280,256]{2,1,0:T(8,128)(2,1)} %refs_0_.11, bf16[1280,128]{1,0:T(8,128)(2,1)S(1)} %get-tuple-element.222.refs_1_, f32[256,128]{1,0:T(8,128)} %get-tuple-element.223.refs_2_), custom_call_target="tpu_custom_call" | custom-call | flops 1 | bytes 1 | tf_op jit(solution)/shard_map/stratum0_at0/pallas_call | solution.py:324
  10.1 1.7 %collective-permute-start.46 = (f32[648,128]{1,0:T(8,128)S(1)}, f32[648,128]{1,0:T(8,128)S(1)}, u32[]{:S(2)}, u32[]{:S(2)}) collective-permute-start(f32[648,128]{1,0:T(8,128)S(1)} %get-tuple-element.229.refs_1_), channel_id=1, source_target_pairs={{0,1},{1,0},{2,3},{3,2},{4,5},{5,4},{6,7},{7,6},{8,9},{9,8},{10,11... | collective-permute-start | bytes 995336 | tf_op jit(solution)/shard_map/ppermute | solution.py:424
  11.8 1.4 %stratum0_at640.1 = (f32[640,128]{1,0:T(8,128)S(1)}, f32[264,128]{1,0:T(8,128)S(1)}) custom-call(bf16[3,1280,256]{2,1,0:T(8,128)(2,1)} %refs_0_.11, bf16[1280,128]{1,0:T(8,128)(2,1)S(1)} %get-tuple-element.222.refs_1_, f32[256,128]{1,0:T(8,128)S(1)} %get-tuple-element.224.refs_2_, bf16[256,128]{1,0:T(8,128)(2,1)S(1)} %get-tuple-element.225.refs_3_, ...), custom_call_target="tpu_custom_call" | custom-call | flops 1 | bytes 1 | tf_op jit(solution)/shard_map/stratum0_at640/pallas_call | solution.py:324
  13.2 0.4 collective-permute-start.45
  13.7 7.0 %conditional.4 = (f32[264,128]{1,0:T(8,128)}) conditional(s32[]{:T(128)} %bitcast.1, f32[264,128]{1,0:T(8,128)S(1)} %get-tuple-element.231, f32[264,128]{1,0:T(8,128)S(1)} %get-tuple-element.231, f32[264,128]{1,0:T(8,128)S(1)} %get-tuple-element.231, f32[264,128]{1,0:T(8,128)S(1)} %get-tuple-element.231, ...), branch_computations={%region_15.0_spmd, %region_16.0_spmd, %region_17.0_spmd, %region_1... | conditional | bytes 540720 | solution.py:433
  13.7 3.8 %collective-permute-start.26 = (f32[264,128]{1,0:T(8,128)S(1)}, f32[264,128]{1,0:T(8,128)}, u32[]{:S(2)}, u32[]{:S(2)}) collective-permute-start(f32[264,128]{1,0:T(8,128)S(1)} %param.26), channel_id=1, source_target_pairs={{0,24},{2,26},{4,28},{6,30},{8,16},{10,18},{12,20},{14,22},{16,8},... | collective-permute-start | bytes 405512 | tf_op jit(solution)/shard_map/cond/branch_11_fun/ppermute | solution.py:424
  17.4 3.3 %collective-permute-done.26 = f32[264,128]{1,0:T(8,128)} collective-permute-done((f32[264,128]{1,0:T(8,128)S(1)}, f32[264,128]{1,0:T(8,128)}, u32[]{:S(2)}, u32[]{:S(2)}) %collective-permute-start.26) | collective-permute-done | bytes 135200 | tf_op jit(solution)/shard_map/cond/branch_11_fun/ppermute | solution.py:424
  20.7 0.2 collective-permute-done.46.refs_2_
  20.9 0.0 copy-done
  20.9 2.0 %stratum1_at0.1 = (f32[648,128]{1,0:T(8,128)S(1)}, f32[640,128]{1,0:T(8,128)S(1)}, f32[8,128]{1,0:T(8,128)S(1)}, bf16[256,128]{1,0:T(8,128)(2,1)S(1)}, f32[264,1...) custom-call(bf16[3,1280,256]{2,1,0:T(8,128)(2,1)} %refs_0_.11, ...), custom_call_target="tpu_custom_call" | custom-call | flops 1 | bytes 1 | tf_op jit(solution)/shard_map/stratum1_at0/pallas_call | solution.py:324
  22.9 1.7 %collective-permute-start.48 = (f32[648,128]{1,0:T(8,128)S(1)}, f32[648,128]{1,0:T(8,128)S(1)}, u32[]{:S(2)}, u32[]{:S(2)}) collective-permute-start(f32[648,128]{1,0:T(8,128)S(1)} %get-tuple-element.239.refs_1_), channel_id=1, source_target_pairs={{0,1},{1,0},{2,3},{3,2},{4,5},{5,4},{6,7},{7,6},{8,9},{9,8},{10,11... | collective-permute-start | bytes 995336 | tf_op jit(solution)/shard_map/ppermute | solution.py:424
  24.6 3.3 %collective-permute-done.45.refs_2_ = f32[640,128]{1,0:T(8,128)S(1)} collective-permute-done((f32[640,128]{1,0:T(8,128)S(1)}, f32[640,128]{1,0:T(8,128)S(1)}, u32[]{:S(2)}, u32[]{:S(2)}) %collective-permute-start.45) | collective-permute-done | bytes 327712 | tf_op jit(solution)/shard_map/ppermute | solution.py:424
  27.9 1.4 %stratum1_at640.1 = (f32[640,128]{1,0:T(8,128)S(1)}, f32[640,128]{1,0:T(8,128)S(1)}, f32[264,128]{1,0:T(8,128)S(1)}) custom-call(bf16[3,1280,256]{2,1,0:T(8,128)(2,1)} %refs_0_.11, f32[640,128]{1,0:T(8,128)S(1)} %get-tuple-element.228.refs_1_, f32[640,128]{1,0:T(8,128)S(1)} %collective-permute-done.45.refs_2_, bf16[1280,128]{1,0:T(8,128)(2,1)S(1)} %copy-done, ...), custom_call_target="tpu_custom_call" | custom-call | flops 1 | bytes 1 | tf_op jit(solution)/shard_map/stratum1_at640/pallas_call | solution.py:324
  29.3 1.7 %collective-permute-start.47 = (f32[640,128]{1,0:T(8,128)S(1)}, f32[640,128]{1,0:T(8,128)S(1)}, u32[]{:S(2)}, u32[]{:S(2)}) collective-permute-start(f32[640,128]{1,0:T(8,128)S(1)} %get-tuple-element.237.refs_1_), channel_id=1, source_target_pairs={{0,1},{1,0},{2,3},{3,2},{4,5},{5,4},{6,7},{7,6},{8,9},{9,8},{10,11... | collective-permute-start | bytes 983048 | tf_op jit(solution)/shard_map/ppermute | solution.py:424
  31.0 6.7 %conditional.5 = (f32[264,128]{1,0:T(8,128)}) conditional(s32[]{:T(128)} %bitcast.2, f32[264,128]{1,0:T(8,128)S(1)} %get-tuple-element.242, f32[264,128]{1,0:T(8,128)S(1)} %get-tuple-element.242, f32[264,128]{1,0:T(8,128)S(1)} %get-tuple-element.242, f32[264,128]{1,0:T(8,128)S(1)} %get-tuple-element.242, ...), branch_computations={%region_30.0_spmd, %region_31.0_spmd, %region_32.0_spmd, %region_3... | conditional | bytes 540720 | solution.py:433
  31.1 0.0 collective-permute-start.36
  31.1 6.7 %collective-permute-done.36 = f32[264,128]{1,0:T(8,128)} collective-permute-done((f32[264,128]{1,0:T(8,128)S(1)}, f32[264,128]{1,0:T(8,128)}, u32[]{:S(2)}, u32[]{:S(2)}) %collective-permute-start.36) | collective-permute-done | bytes 135200 | tf_op jit(solution)/shard_map/cond/branch_6_fun/ppermute | solution.py:424
  37.8 0.0 collective-permute-done.48.refs_2_
  37.8 1.8 %stratum2_at0.1 = (f32[648,128]{1,0:T(8,128)S(1)}, f32[640,128]{1,0:T(8,128)S(1)}, f32[8,128]{1,0:T(8,128)S(1)}, bf16[256,128]{1,0:T(8,128)(2,1)S(1)}, f32[264,1...) custom-call(bf16[3,1280,256]{2,1,0:T(8,128)(2,1)} %refs_0_.11, ...), custom_call_target="tpu_custom_call" | custom-call | flops 1 | bytes 1 | tf_op jit(solution)/shard_map/stratum2_at0/pallas_call | solution.py:324
  39.6 0.4 collective-permute-start.50
  39.9 0.4 collective-permute-done.47.refs_2_
  40.3 1.4 %stratum2_at640.1 = (f32[384,128]{1,0:T(8,128)S(1)}, f32[256,128]{1,0:T(8,128)S(1)}, f32[640,128]{1,0:T(8,128)S(1)}, f32[264,128]{1,0:T(8,128)S(1)}) custom-call(bf16[3,1280,256]{2,1,0:T(8,128)(2,1)} %refs_0_.11, f32[640,128]{1,0:T(8,128)S(1)} %get-tuple-element.237.refs_1_, f32[640,128]{1,0:T(8,128)S(1)} %collective-permute-done.47.refs_2_, ...), custom_call_target="tpu_custom_call" | custom-call | flops 1 | bytes 1 | tf_op jit(solution)/shard_map/stratum2_at640/pallas_call | solution.py:324
  41.7 1.4 %collective-permute-start.51 = (f32[384,128]{1,0:T(8,128)S(1)}, f32[384,128]{1,0:T(8,128)S(1)}, u32[]{:S(2)}, u32[]{:S(2)}) collective-permute-start(f32[384,128]{1,0:T(8,128)S(1)} %get-tuple-element.253.refs_0_), channel_id=1, source_target_pairs={{0,1},{1,0},{2,3},{3,2},{4,5},{5,4},{6,7},{7,6},{8,9},{9,8},{10,11... | collective-permute-start | bytes 589832 | tf_op jit(solution)/shard_map/ppermute | solution.py:424
  43.1 1.9 %collective-permute-start.52 = (f32[264,128]{1,0:T(8,128)S(1)}, f32[264,128]{1,0:T(8,128)S(1)}, u32[]{:S(2)}, u32[]{:S(2)}) collective-permute-start(f32[264,128]{1,0:T(8,128)S(1)} %get-tuple-element.255), channel_id=1, source_target_pairs={{0,30},{2,28},{4,26},{6,24},{8,22},{10,20},{12,18},{14,16},{16,14}... | collective-permute-start | bytes 405512 | tf_op jit(solution)/shard_map/ppermute | solution.py:424
  45.0 0.5 collective-permute-start.49
  45.6 4.7 %collective-permute-done.50.refs_1_ = f32[648,128]{1,0:T(8,128)S(1)} collective-permute-done((f32[648,128]{1,0:T(8,128)S(1)}, f32[648,128]{1,0:T(8,128)S(1)}, u32[]{:S(2)}, u32[]{:S(2)}) %collective-permute-start.50) | collective-permute-done | bytes 331808 | tf_op jit(solution)/shard_map/ppermute | solution.py:424
  50.3 1.5 %user_log_at0.1 = (bf16[1280,128]{1,0:T(8,128)(2,1)}, f32[8,128]{1,0:T(8,128)S(1)}) custom-call(f32[648,128]{1,0:T(8,128)S(1)} %get-tuple-element.250.refs_0_, f32[648,128]{1,0:T(8,128)S(1)} %collective-permute-done.50.refs_1_, f32[640,128]{1,0:T(8,128)S(1)} %get-tuple-element.251.refs_2_, f32[8,128]{1,0:T(8,128)S(1)} %get-tuple-element.243.refs_4_.refs_3_), custom_call_target="tpu_custom_call" | custom-call | flops 3276800 | bytes 1146880 | tf_op jit(solution)/shard_map/user_log_at0/pallas_call | solution.py:381
  51.8 0.0 collective-permute-done.52.item
  51.8 0.9 %item_log.1 = bf16[256,128]{1,0:T(8,128)(2,1)} custom-call(f32[264,128]{1,0:T(8,128)S(1)} %collective-permute-done.52.item, f32[8,128]{1,0:T(8,128)S(1)} %get-tuple-element.252.refs_3_._), custom_call_target="tpu_custom_call" | custom-call | flops 1310720 | bytes 196608 | tf_op jit(solution)/shard_map/item_log/pallas_call | solution.py:411
  52.7 1.8 %collective-permute-done.51.refs_1_ = f32[384,128]{1,0:T(8,128)S(1)} collective-permute-done((f32[384,128]{1,0:T(8,128)S(1)}, f32[384,128]{1,0:T(8,128)S(1)}, u32[]{:S(2)}, u32[]{:S(2)}) %collective-permute-start.51) | collective-permute-done | bytes 196640 | tf_op jit(solution)/shard_map/ppermute | solution.py:424
  54.5 1.1 %user_log_at640.1.refs_4_ = bf16[1280,128]{1,0:T(8,128)(2,1)} custom-call(f32[384,128]{1,0:T(8,128)S(1)} %get-tuple-element.253.refs_0_, f32[384,128]{1,0:T(8,128)S(1)} %collective-permute-done.51.refs_1_, f32[640,128]{1,0:T(8,128)S(1)} %get-tuple-element.249.refs_2_, f32[8,128]{1,0:T(8,128)S(1)} %get-tuple-element.252.refs_3_._, ...), custom_call_target="tpu_custom_call", output_to_operand_aliasing={{}: (4, {})} | custom-call | flops 1966080 | bytes 688128 | tf_op jit(solution)/shard_map/user_log_at640/pallas_call | solution.py:381
  55.6 0.9 %collective-permute-done.49.refs_1_ = f32[256,128]{1,0:T(8,128)S(1)} collective-permute-done((f32[256,128]{1,0:T(8,128)S(1)}, f32[256,128]{1,0:T(8,128)S(1)}, u32[]{:S(2)}, u32[]{:S(2)}) %collective-permute-start.49) | collective-permute-done | bytes 131104 | tf_op jit(solution)/shard_map/ppermute | solution.py:424
  56.5 1.0 %user_log_at1024.1 = bf16[1280,128]{1,0:T(8,128)(2,1)} custom-call(f32[256,128]{1,0:T(8,128)S(1)} %get-tuple-element.248.refs_0_, f32[256,128]{1,0:T(8,128)S(1)} %collective-permute-done.49.refs_1_, f32[640,128]{1,0:T(8,128)S(1)} %get-tuple-element.249.refs_2_, f32[8,128]{1,0:T(8,128)S(1)} %get-tuple-element.252.refs_3_._, ...), custom_call_target="tpu_custom_call", output_to_operand_aliasing={{}: (4, {})} | custom-call | flops 1310720 | bytes 458752 | tf_op jit(solution)/shard_map/user_log_at1024/pallas_call | solution.py:381
Async XLA Ops:
  1.6 6.7 %collective-permute-start.3 = (f32[256,128]{1,0:T(8,128)S(1)}, f32[256,128]{1,0:T(8,128)}, u32[]{:S(2)}, u32[]{:S(2)}) collective-permute-start(f32[256,128]{1,0:T(8,128)S(1)} %get-tuple-element.134), channel_id=1, source_target_pairs={{0,8},{2,10},{4,12},{6,14},{8,0},{10,2},{12,4},{14,6},{16,24},{18,... | collective-permute-start | bytes 393224 | tf_op jit(solution)/shard_map/cond/branch_3_fun/ppermute | solution.py:424
  8.2 12.6 %copy-start = (bf16[1280,128]{1,0:T(8,128)(2,1)S(1)}, bf16[1280,128]{1,0:T(8,128)(2,1)}, u32[]{:S(2)}) copy-start(bf16[1280,128]{1,0:T(8,128)(2,1)} %refs_3_.3) | copy-start | bytes 983044
  10.1 10.8 %collective-permute-start.46 = (f32[648,128]{1,0:T(8,128)S(1)}, f32[648,128]{1,0:T(8,128)S(1)}, u32[]{:S(2)}, u32[]{:S(2)}) collective-permute-start(f32[648,128]{1,0:T(8,128)S(1)} %get-tuple-element.229.refs_1_), channel_id=1, source_target_pairs={{0,1},{1,0},{2,3},{3,2},{4,5},{5,4},{6,7},{7,6},{8,9},{9,8},{10,11... | collective-permute-start | bytes 995336 | tf_op jit(solution)/shard_map/ppermute | solution.py:424
  13.2 14.7 %collective-permute-start.45 = (f32[640,128]{1,0:T(8,128)S(1)}, f32[640,128]{1,0:T(8,128)S(1)}, u32[]{:S(2)}, u32[]{:S(2)}) collective-permute-start(f32[640,128]{1,0:T(8,128)S(1)} %get-tuple-element.228.refs_1_), channel_id=1, source_target_pairs={{0,1},{1,0},{2,3},{3,2},{4,5},{5,4},{6,7},{7,6},{8,9},{9,8},{10,11... | collective-permute-start | bytes 983048 | tf_op jit(solution)/shard_map/ppermute | solution.py:424
  13.7 7.0 %collective-permute-start.26 = (f32[264,128]{1,0:T(8,128)S(1)}, f32[264,128]{1,0:T(8,128)}, u32[]{:S(2)}, u32[]{:S(2)}) collective-permute-start(f32[264,128]{1,0:T(8,128)S(1)} %param.26), channel_id=1, source_target_pairs={{0,24},{2,26},{4,28},{6,30},{8,16},{10,18},{12,20},{14,22},{16,8},... | collective-permute-start | bytes 405512 | tf_op jit(solution)/shard_map/cond/branch_11_fun/ppermute | solution.py:424
  22.9 14.9 %collective-permute-start.48 = (f32[648,128]{1,0:T(8,128)S(1)}, f32[648,128]{1,0:T(8,128)S(1)}, u32[]{:S(2)}, u32[]{:S(2)}) collective-permute-start(f32[648,128]{1,0:T(8,128)S(1)} %get-tuple-element.239.refs_1_), channel_id=1, source_target_pairs={{0,1},{1,0},{2,3},{3,2},{4,5},{5,4},{6,7},{7,6},{8,9},{9,8},{10,11... | collective-permute-start | bytes 995336 | tf_op jit(solution)/shard_map/ppermute | solution.py:424
  29.3 11.0 %collective-permute-start.47 = (f32[640,128]{1,0:T(8,128)S(1)}, f32[640,128]{1,0:T(8,128)S(1)}, u32[]{:S(2)}, u32[]{:S(2)}) collective-permute-start(f32[640,128]{1,0:T(8,128)S(1)} %get-tuple-element.237.refs_1_), channel_id=1, source_target_pairs={{0,1},{1,0},{2,3},{3,2},{4,5},{5,4},{6,7},{7,6},{8,9},{9,8},{10,11... | collective-permute-start | bytes 983048 | tf_op jit(solution)/shard_map/ppermute | solution.py:424
  31.1 6.7 %collective-permute-start.36 = (f32[264,128]{1,0:T(8,128)S(1)}, f32[264,128]{1,0:T(8,128)}, u32[]{:S(2)}, u32[]{:S(2)}) collective-permute-start(f32[264,128]{1,0:T(8,128)S(1)} %param.36), channel_id=1, source_target_pairs={{0,14},{2,12},{4,10},{6,8},{8,6},{10,4},{12,2},{14,0},{16,30},{18,... | collective-permute-start | bytes 405512 | tf_op jit(solution)/shard_map/cond/branch_6_fun/ppermute | solution.py:424
  39.6 10.7 %collective-permute-start.50 = (f32[648,128]{1,0:T(8,128)S(1)}, f32[648,128]{1,0:T(8,128)S(1)}, u32[]{:S(2)}, u32[]{:S(2)}) collective-permute-start(f32[648,128]{1,0:T(8,128)S(1)} %get-tuple-element.250.refs_0_), channel_id=1, source_target_pairs={{0,1},{1,0},{2,3},{3,2},{4,5},{5,4},{6,7},{7,6},{8,9},{9,8},{10,11... | collective-permute-start | bytes 995336 | tf_op jit(solution)/shard_map/ppermute | solution.py:424
  41.7 12.8 %collective-permute-start.51 = (f32[384,128]{1,0:T(8,128)S(1)}, f32[384,128]{1,0:T(8,128)S(1)}, u32[]{:S(2)}, u32[]{:S(2)}) collective-permute-start(f32[384,128]{1,0:T(8,128)S(1)} %get-tuple-element.253.refs_0_), channel_id=1, source_target_pairs={{0,1},{1,0},{2,3},{3,2},{4,5},{5,4},{6,7},{7,6},{8,9},{9,8},{10,11... | collective-permute-start | bytes 589832 | tf_op jit(solution)/shard_map/ppermute | solution.py:424
  43.1 8.6 %collective-permute-start.52 = (f32[264,128]{1,0:T(8,128)S(1)}, f32[264,128]{1,0:T(8,128)S(1)}, u32[]{:S(2)}, u32[]{:S(2)}) collective-permute-start(f32[264,128]{1,0:T(8,128)S(1)} %get-tuple-element.255), channel_id=1, source_target_pairs={{0,30},{2,28},{4,26},{6,24},{8,22},{10,20},{12,18},{14,16},{16,14}... | collective-permute-start | bytes 405512 | tf_op jit(solution)/shard_map/ppermute | solution.py:424
  45.0 11.4 %collective-permute-start.49 = (f32[256,128]{1,0:T(8,128)S(1)}, f32[256,128]{1,0:T(8,128)S(1)}, u32[]{:S(2)}, u32[]{:S(2)}) collective-permute-start(f32[256,128]{1,0:T(8,128)S(1)} %get-tuple-element.248.refs_0_), channel_id=1, source_target_pairs={{0,1},{1,0},{2,3},{3,2},{4,5},{5,4},{6,7},{7,6},{8,9},{9,8},{10,11... | collective-permute-start | bytes 393224 | tf_op jit(solution)/shard_map/ppermute | solution.py:424
